TPU v7x, 32 devices: a whole 2x2x4 slice. The times are simulated.
32 devices in a mesh: seq: 16 (over z, y, core), row: 2 (over x).
Axes of the slice: x: 2, y: 2, z: 4, core: 2. Of those that a mesh axis runs over, the one named last changes fastest.
Arguments:
- tokens: bfloat16 [2, 8192, 768], P('row', 'seq'), may hold values from -18 to 18
- cotangent: bfloat16 [2, 8192, 768], P('row', 'seq'), may hold values from -6 to 6
- lengths: int32 [2, 4], P('row'), may hold values from 1 to 7681, 8192 in all within a row
- padding: int32 [2, 8192], P('row', 'seq'), may hold values 0 or 1
- feature_draws: float32 [12, 64, 64], replicated, may hold values from -4 to 4
- rel_bias: float32 [12, 1024], replicated, may hold values from -4 to 4
- w_qkv: bfloat16 [768, 2304], P(('seq', 'row')), may hold values from -0.21875 to 0.21875
- b_qkv: bfloat16 [2304], P(('seq', 'row')), may hold values from -1.5 to 1.5
- w_out: bfloat16 [768, 768], P(('seq', 'row')), may hold values from -1.25 to 1.25
- b_out: bfloat16 [768], P(('seq', 'row')), may hold values from -1.5 to 1.5
- gain_attn: bfloat16 [768], P(('seq', 'row')), may hold values from 0.5 to 1.5
- shift_attn: bfloat16 [768], P(('seq', 'row')), may hold values from -1.5 to 1.5
- w_up: bfloat16 [768, 3072], P(('seq', 'row')), may hold values from -0.21875 to 0.21875
- b_up: bfloat16 [3072], P(('seq', 'row')), may hold values from -1.5 to 1.5
- w_down: bfloat16 [3072, 768], P(('seq', 'row')), may hold values from -0.109375 to 0.109375
- b_down: bfloat16 [768], P(('seq', 'row')), may hold values from -1.5 to 1.5
- gain_ffn: bfloat16 [768], P(('seq', 'row')), may hold values from 0.5 to 1.5
- shift_ffn: bfloat16 [768], P(('seq', 'row')), may hold values from -1.5 to 1.5
Outputs:
- output: bfloat16 [2, 8192, 768], P('row', 'seq')
- grad_tokens: float32 [2, 8192, 768], P('row', 'seq')
- grad_rel_bias: float32 [12, 1024], replicated
- grad_qkv: float32 [768, 2304], P(('seq', 'row'))
- grad_qkv_bias: float32 [2304], P(('seq', 'row'))
- grad_out: float32 [768, 768], P(('seq', 'row'))
- grad_out_bias: float32 [768], P(('seq', 'row'))
- grad_gain_attn: float32 [768], P(('seq', 'row'))
- grad_shift_attn: float32 [768], P(('seq', 'row'))
- grad_up: float32 [768, 3072], P(('seq', 'row'))
- grad_up_bias: float32 [3072], P(('seq', 'row'))
- grad_down: float32 [3072, 768], P(('seq', 'row'))
- grad_down_bias: float32 [768], P(('seq', 'row'))
- gradient_feedforward_gain: float32 [768], P(('seq', 'row'))
- grad_shift_ffn: float32 [768], P(('seq', 'row'))
Inputs may be any that keep to these rules, and one draw needn't show every extreme that they name: Each row's lengths sum to 8192, and its longest document has exactly 7681 tokens.
All inputs are finite; a program needn't handle non-finite values. No bound on the sum of `padding` on one device may be relied on, other than what follows from the above.
Results may differ from a plain program's by a relative error of at most 0.017.
Values may be sent and summed in bfloat16 or wider, within the bound.
A program may use at most 192 MiB of HBM per device.

v0:
```python
from functools import partial

import jax
import jax.numpy as jnp
from jax import lax
from jax.sharding import PartitionSpec as P

EPS = 1e-06
EXACT_MATMUL = lax.Precision.HIGHEST


def padded_2(cells, sides, width):
    for axis, dim in sides:
        count = lax.axis_size(axis)
        ends = count - 1
        head = lax.slice_in_dim(cells, 0, width, axis=dim)
        tail = lax.slice_in_dim(cells, cells.shape[dim] - width, cells.shape[dim], axis=dim)
        cells = jnp.concatenate(
            [
                lax.ppermute(tail, axis, [(i, (i + 1) % count) for i in range(ends)]),
                cells,
                lax.ppermute(head, axis, [((i + 1) % count, i) for i in range(ends)]),
            ],
            axis=dim,
        )
    return cells


def passed_along(block, axis, distance):
    devices = range(lax.axis_size(axis))
    route = [(i - distance, i) for i in devices if i - distance in devices]
    return lax.ppermute(block, axis, route)


def layer_norm(values, gain, shift):
    center = values - jnp.mean(values, -1, keepdims=True)
    spread = jnp.mean(center * center, -1, keepdims=True)
    return center * lax.rsqrt(spread + EPS) * gain + shift


def feature_map(heads_in, random_features):
    scaled_input = heads_in * heads_in.shape[-1] ** (-0.25)
    projected_rows = jnp.einsum(
        "ykb,kib->yki", scaled_input, random_features, precision=EXACT_MATMUL
    )
    half_square = 0.5 * jnp.sum(scaled_input * scaled_input, -1, keepdims=True)
    return jnp.exp(projected_rows - half_square) * random_features.shape[1] ** (-0.5)


def toeplitz(rows_in, q_block):
    head_count, window_len = rows_in.shape
    key_span = q_block + window_len
    padded = jnp.pad(rows_in, ((0, 0), (0, key_span + 1 - window_len)))
    tiled = jnp.broadcast_to(padded[:, None, :], (head_count, q_block, key_span + 1))
    tiled = tiled.reshape(head_count, q_block * (key_span + 1))
    return tiled[:, : q_block * key_span].reshape(head_count, q_block, key_span)


def diagonal_sums(matrix, window_len):
    head_count, q_block, key_span = matrix.shape
    flat = jnp.pad(matrix.reshape(head_count, q_block * key_span), ((0, 0), (0, q_block)))
    return jnp.sum(flat.reshape(head_count, q_block, key_span + 1)[:, :, :window_len], 1)


def document_numbers(positions, lengths_row):
    ends = jnp.cumsum(lengths_row)
    counted = jnp.sum((positions[:, None] >= ends[None, :]).astype(jnp.int32), -1)
    return jnp.where(positions < 0, -1, counted)


def band_mask(doc_query, doc_keys, pad_keys, half_win):
    row_count = doc_query.shape[0]
    col_count = doc_keys.shape[0]
    diagonal = (
        jnp.arange(col_count, dtype=jnp.int32)[None, :]
        == jnp.arange(row_count, dtype=jnp.int32)[:, None] + half_win
    )
    same_doc = doc_query[:, None] == doc_keys[None, :]
    return jnp.where(same_doc & ((pad_keys[None, :] == 1) | diagonal), 1.0, 0.0).astype(jnp.float32)


def take_head(array, head):
    return lax.dynamic_index_in_dim(array, head, 1, keepdims=False)


def on_device(
    tokens,
    cotangent,
    lengths,
    padding,
    feature_draws,
    rel_bias,
    w_qkv,
    b_qkv,
    w_out,
    b_out,
    gain_attn,
    shift_attn,
    w_up,
    b_up,
    w_down,
    b_down,
    gain_ffn,
    shift_ffn,
):
    local = tokens[0]
    seq_len = local.shape[0]
    model_width = local.shape[1]
    head_count = rel_bias.shape[0]
    window_len = rel_bias.shape[1]
    half_win = window_len // 2
    feat_count = feature_draws.shape[1]
    head_dim = model_width // head_count
    feat_cols = head_count * feat_count
    q_block = min(512, seq_len)
    block_count = seq_len // q_block
    key_span = q_block + window_len
    exp_bias = jnp.exp(rel_bias)
    params = (
        lax.all_gather(w_qkv, ("seq", "row"), axis=0, tiled=True),
        lax.all_gather(b_qkv, ("seq", "row"), axis=0, tiled=True),
        lax.all_gather(w_out, ("seq", "row"), axis=0, tiled=True),
        lax.all_gather(b_out, ("seq", "row"), axis=0, tiled=True),
        lax.all_gather(gain_attn, ("seq", "row"), axis=0, tiled=True),
        lax.all_gather(shift_attn, ("seq", "row"), axis=0, tiled=True),
        lax.all_gather(w_up, ("seq", "row"), axis=0, tiled=True),
        lax.all_gather(b_up, ("seq", "row"), axis=0, tiled=True),
        lax.all_gather(w_down, ("seq", "row"), axis=0, tiled=True),
        lax.all_gather(b_down, ("seq", "row"), axis=0, tiled=True),
        lax.all_gather(gain_ffn, ("seq", "row"), axis=0, tiled=True),
        lax.all_gather(shift_ffn, ("seq", "row"), axis=0, tiled=True),
    )
    (
        qkv_w,
        qkv_b,
        out_w,
        out_b,
        first_norm_gain,
        shift_one,
        up_w,
        up_b,
        down_w,
        down_b,
        gain_two,
        shift_two,
    ) = params
    seq_pos = lax.axis_index("seq")
    start_pos = seq_pos * seq_len
    positions = start_pos + jnp.arange(seq_len, dtype=jnp.int32)
    ext_pos = start_pos - half_win + jnp.arange(seq_len + window_len, dtype=jnp.int32)
    doc_query = document_numbers(positions, lengths[0])
    doc_keys = document_numbers(ext_pos, lengths[0])
    pad_local = padding[0]
    pad_ones = jnp.ones((half_win,), jnp.int32)
    pad_keys = jnp.concatenate([pad_ones, pad_local, pad_ones])
    proj_qkv = jnp.dot(local, qkv_w, preferred_element_type=jnp.float32) + qkv_b
    queries = proj_qkv[:, :model_width].reshape(seq_len, head_count, head_dim)
    keys_in = proj_qkv[:, model_width : 2 * model_width].reshape(seq_len, head_count, head_dim)
    q_full, query_back = jax.vjp(partial(feature_map, random_features=feature_draws), queries)
    k_full, key_back = jax.vjp(partial(feature_map, random_features=feature_draws), keys_in)
    q_feat = q_full.astype(jnp.bfloat16)
    k_flat = k_full.astype(jnp.bfloat16).reshape(seq_len, feat_cols)
    values_low = proj_qkv[:, 2 * model_width :].astype(jnp.bfloat16)
    own_keys = jnp.concatenate([k_flat, values_low], 1)
    masked_keys = jnp.concatenate([k_flat * pad_local.astype(jnp.bfloat16)[:, None], values_low], 1)
    rims = padded_2(masked_keys, (("seq", 0),), half_win)
    key_ext = jnp.concatenate([rims[:half_win], own_keys, rims[half_win + seq_len :]], 0)

    def window_of():
        keys_w = key_ext[:, :feat_cols].reshape(key_span, head_count, feat_count)
        values_w = key_ext[:, feat_cols:].reshape(key_span, head_count, head_dim)
        mask = band_mask(doc_query, doc_keys, pad_keys, half_win)
        return (q_feat, keys_w, values_w, mask)

    def head_coef(head):
        return toeplitz(lax.dynamic_slice_in_dim(exp_bias, head, 1, 0), q_block)[0]

    def attend(start):
        fq_blk, keys_w, values_w, mask = window_of()

        def per_head(head):
            fq_head = take_head(fq_blk, head)
            keys_head = take_head(keys_w, head)
            score = jnp.einsum("qm,km->qk", fq_head, keys_head, preferred_element_type=jnp.float32)
            weight = score * head_coef(head) * mask
            totals = jnp.sum(weight, -1)
            weighted = jnp.dot(
                weight.astype(jnp.bfloat16),
                take_head(values_w, head),
                preferred_element_type=jnp.float32,
            )
            return (weighted / totals[:, None], totals)

        return lax.map(per_head, jnp.arange(head_count, dtype=jnp.int32))

    starts = jnp.arange(block_count, dtype=jnp.int32) * q_block
    att_heads, totals_all = lax.map(attend, starts)
    attended = att_heads.transpose(0, 2, 1, 3).reshape(seq_len, model_width)
    att_low = attended.astype(jnp.bfloat16)
    branch = jnp.dot(att_low, out_w, preferred_element_type=jnp.float32) + out_b
    resid_one = local.astype(jnp.float32) + branch
    hidden_one, ln_one_back = jax.vjp(
        layer_norm, resid_one, first_norm_gain.astype(jnp.float32), shift_one.astype(jnp.float32)
    )
    hidden_low = hidden_one.astype(jnp.bfloat16)
    inner = jnp.dot(hidden_low, up_w, preferred_element_type=jnp.float32) + up_b
    active, gelu_back = jax.vjp(partial(jax.nn.gelu, approximate=False), inner)
    active_low = active.astype(jnp.bfloat16)
    ffn_out = jnp.dot(active_low, down_w, preferred_element_type=jnp.float32) + down_b
    result, ln_two_back = jax.vjp(
        layer_norm,
        hidden_one + ffn_out,
        gain_two.astype(jnp.float32),
        shift_two.astype(jnp.float32),
    )
    params = (
        lax.all_gather(w_qkv, ("seq", "row"), axis=0, tiled=True),
        lax.all_gather(b_qkv, ("seq", "row"), axis=0, tiled=True),
        lax.all_gather(w_out, ("seq", "row"), axis=0, tiled=True),
        lax.all_gather(b_out, ("seq", "row"), axis=0, tiled=True),
        lax.all_gather(gain_attn, ("seq", "row"), axis=0, tiled=True),
        lax.all_gather(shift_attn, ("seq", "row"), axis=0, tiled=True),
        lax.all_gather(w_up, ("seq", "row"), axis=0, tiled=True),
        lax.all_gather(b_up, ("seq", "row"), axis=0, tiled=True),
        lax.all_gather(w_down, ("seq", "row"), axis=0, tiled=True),
        lax.all_gather(b_down, ("seq", "row"), axis=0, tiled=True),
        lax.all_gather(gain_ffn, ("seq", "row"), axis=0, tiled=True),
        lax.all_gather(shift_ffn, ("seq", "row"), axis=0, tiled=True),
    )
    (
        qkv_w,
        qkv_b,
        out_w,
        out_b,
        first_norm_gain,
        shift_one,
        up_w,
        up_b,
        down_w,
        down_b,
        gain_two,
        shift_two,
    ) = params
    grad_two, grad_gain_two, grad_shift_two = ln_two_back(cotangent[0].astype(jnp.float32))
    grad_two_low = grad_two.astype(jnp.bfloat16)
    grad_down_w = jnp.einsum(
        "ti,tj->ij", active_low, grad_two_low, preferred_element_type=jnp.float32
    )
    grad_down_b = jnp.sum(grad_two_low, 0, dtype=jnp.float32)
    grad_active = jnp.dot(grad_two_low, down_w.T, preferred_element_type=jnp.float32)
    grad_inner_low = gelu_back(grad_active)[0].astype(jnp.bfloat16)
    grad_up_w = jnp.einsum(
        "ti,tj->ij", hidden_low, grad_inner_low, preferred_element_type=jnp.float32
    )
    grad_up_b = jnp.sum(grad_inner_low, 0, dtype=jnp.float32)
    grad_hidden = grad_two + jnp.dot(grad_inner_low, up_w.T, preferred_element_type=jnp.float32)
    grad_one, grad_gain_one, grad_shift_one = ln_one_back(grad_hidden)
    grad_one_low = grad_one.astype(jnp.bfloat16)
    grad_out_w = jnp.einsum("ti,tj->ij", att_low, grad_one_low, preferred_element_type=jnp.float32)
    grad_out_b = jnp.sum(grad_one_low, 0, dtype=jnp.float32)
    grad_att = jnp.dot(grad_one_low, out_w.T, preferred_element_type=jnp.float32)
    grad_att_heads = grad_att.reshape(block_count, q_block, head_count, head_dim).transpose(
        0, 2, 1, 3
    )

    def back_block(carry, inputs):
        grad_kf, grad_vv, grad_bias = carry
        start, grad_att_blk, att_blk, totals_blk = inputs
        fq_blk, keys_w, values_w, mask = window_of()

        def per_head_back(head):
            fq_head = take_head(fq_blk, head)
            keys_head = take_head(keys_w, head)
            values_head = take_head(values_w, head)
            coef_head = head_coef(head)
            score = jnp.einsum("qm,km->qk", fq_head, keys_head, preferred_element_type=jnp.float32)
            weight = score * coef_head * mask
            inverse = 1.0 / totals_blk[head]
            grad_head = grad_att_blk[head]
            grad_weighted = (grad_head * inverse[:, None]).astype(jnp.bfloat16)
            grad_total = -jnp.sum(grad_head * att_blk[head], -1) * inverse
            grad_weight = (
                jnp.einsum(
                    "qd,kd->qk", grad_weighted, values_head, preferred_element_type=jnp.float32
                )
                + grad_total[:, None]
            )
            grad_score = (grad_weight * coef_head * mask).astype(jnp.bfloat16)
            grad_fq = jnp.einsum(
                "qk,km->qm", grad_score, keys_head, preferred_element_type=jnp.float32
            )
            grad_keys_head = jnp.einsum(
                "qk,qm->km", grad_score, fq_head, preferred_element_type=jnp.float32
            )
            grad_values_head = jnp.einsum(
                "qk,qd->kd",
                weight.astype(jnp.bfloat16),
                grad_weighted,
                preferred_element_type=jnp.float32,
            )
            grad_bias_head = diagonal_sums((grad_weight * weight)[None], window_len)[0]
            return (grad_fq, grad_keys_head, grad_values_head, grad_bias_head)

        grad_fq_blk, key_part, value_part, bias_part = lax.map(
            per_head_back, jnp.arange(head_count, dtype=jnp.int32)
        )
        key_part = key_part.transpose(1, 0, 2).reshape(key_span, feat_cols)
        value_part = value_part.transpose(1, 0, 2).reshape(key_span, model_width)
        grad_kf = grad_kf + key_part
        grad_vv = grad_vv + value_part
        return ((grad_kf, grad_vv, grad_bias + bias_part), grad_fq_blk.transpose(1, 0, 2))

    carry_init = (
        jnp.zeros((seq_len + window_len, feat_cols), jnp.float32),
        jnp.zeros((seq_len + window_len, model_width), jnp.float32),
        jnp.zeros((head_count, window_len), jnp.float32),
    )
    (grad_kf, grad_vv, grad_bias), grad_fq_all = lax.scan(
        back_block, carry_init, (starts, grad_att_heads, att_heads, totals_all)
    )
    lower_rim = jnp.concatenate([grad_kf[:half_win], grad_vv[:half_win]], 1)
    upper_rim = jnp.concatenate([grad_kf[half_win + seq_len :], grad_vv[half_win + seq_len :]], 1)
    from_right = passed_along(lower_rim.astype(jnp.bfloat16), "seq", -1).astype(lower_rim.dtype)
    from_left = passed_along(upper_rim.astype(jnp.bfloat16), "seq", 1).astype(upper_rim.dtype)
    returned = from_left + from_right
    pad_float = pad_local.astype(jnp.float32)[:, None]
    grad_kfeat = grad_kf[half_win : half_win + seq_len] + returned[:, :feat_cols] * pad_float
    value_gradient = grad_vv[half_win : half_win + seq_len] + returned[:, feat_cols:]
    grad_queries = query_back(grad_fq_all.reshape(seq_len, head_count, feat_count))[0]
    grad_keys_in = key_back(grad_kfeat.reshape(seq_len, head_count, feat_count))[0]
    grad_proj_low = jnp.concatenate(
        [
            grad_queries.reshape(seq_len, model_width),
            grad_keys_in.reshape(seq_len, model_width),
            value_gradient,
        ],
        1,
    ).astype(jnp.bfloat16)
    grad_qkv_w = jnp.einsum("ti,tj->ij", local, grad_proj_low, preferred_element_type=jnp.float32)
    grad_qkv_b = jnp.sum(grad_proj_low, 0, dtype=jnp.float32)
    grad_input = grad_one + jnp.dot(grad_proj_low, qkv_w.T, preferred_element_type=jnp.float32)
    grad_rel = lax.psum(grad_bias, ("seq", "row"))
    summed = (
        lax.psum_scatter(grad_qkv_w, ("seq", "row"), scatter_dimension=0, tiled=True),
        lax.psum_scatter(grad_qkv_b, ("seq", "row"), scatter_dimension=0, tiled=True),
        lax.psum_scatter(grad_out_w, ("seq", "row"), scatter_dimension=0, tiled=True),
        lax.psum_scatter(grad_out_b, ("seq", "row"), scatter_dimension=0, tiled=True),
        lax.psum_scatter(grad_gain_one, ("seq", "row"), scatter_dimension=0, tiled=True),
        lax.psum_scatter(grad_shift_one, ("seq", "row"), scatter_dimension=0, tiled=True),
        lax.psum_scatter(grad_up_w, ("seq", "row"), scatter_dimension=0, tiled=True),
        lax.psum_scatter(grad_up_b, ("seq", "row"), scatter_dimension=0, tiled=True),
        lax.psum_scatter(grad_down_w, ("seq", "row"), scatter_dimension=0, tiled=True),
        lax.psum_scatter(grad_down_b, ("seq", "row"), scatter_dimension=0, tiled=True),
        lax.psum_scatter(grad_gain_two, ("seq", "row"), scatter_dimension=0, tiled=True),
        lax.psum_scatter(grad_shift_two, ("seq", "row"), scatter_dimension=0, tiled=True),
    )
    return (
        result[None].astype(jnp.bfloat16),
        grad_input[None],
        grad_rel,
        summed[0],
        summed[1],
        summed[2],
        summed[3],
        summed[4],
        summed[5],
        summed[6],
        summed[7],
        summed[8],
        summed[9],
        summed[10],
        summed[11],
    )


def solution(mesh):
    in_specs = (
        P("row", "seq", None),
        P("row", "seq", None),
        P("row", None),
        P("row", "seq"),
        P(),
        P(),
        P(("seq", "row"), None),
        P(("seq", "row")),
        P(("seq", "row"), None),
        P(("seq", "row")),
        P(("seq", "row")),
        P(("seq", "row")),
        P(("seq", "row"), None),
        P(("seq", "row")),
        P(("seq", "row"), None),
        P(("seq", "row")),
        P(("seq", "row")),
        P(("seq", "row")),
    )
    out_specs = (
        P("row", "seq", None),
        P("row", "seq", None),
        P(),
        P(("seq", "row"), None),
        P(("seq", "row")),
        P(("seq", "row"), None),
        P(("seq", "row")),
        P(("seq", "row")),
        P(("seq", "row")),
        P(("seq", "row"), None),
        P(("seq", "row")),
        P(("seq", "row"), None),
        P(("seq", "row")),
        P(("seq", "row")),
        P(("seq", "row")),
    )
    return jax.shard_map(
        on_device, mesh=mesh, in_specs=in_specs, out_specs=out_specs, check_vma=False
    )
```

profile of v0, /device:TPU:0, one launch (start us, length us, event | category | flops | bytes accessed | tf_op | source)
XLA Modules:
  0.0 2972.6 jit_solution(17401960063433923745)
XLA Ops:
  16.8 43.0 %all-reduce.20 = (bf16[2304]{0:T(1024)(128)(2,1)S(1)}, bf16[768]{0:T(1024)(128)(2,1)}, bf16[768]{0:T(1024)(128)(2,1)}, bf16[768]{0:T(1024)(128)(2,1)}, bf16[3072...) all-reduce(bf16[2304]{0:T(1024)(128)(2,1)S(1)} %dynamic-update-slic, ...), channel_id=1, replica_groups=mesh['seq'=16,'row'=2] {'seq','row'}, use_global_device_ids=true, to_apply=%add.3 | all-reduce | flops 9984 | bytes 39936
  61.2 12.7 all-gather.5.cloned.1.call-done
  119.1 674.1 %while.56 = (s32[]{:T(128)}, f32[12,512,64]{1,2,0:T(8,128)}, f32[12,512]{1,0:T(8,128)}, s32[12]{0:T(128)}, bf16[512,12,64]{0,2,1:T(8,128)(2,1)}, /*index=5*/bf16...) while((s32[]{:T(128)}, f32[12,512,64]{1,2,0:T(8,128)}, ...), condition=%wide.region_7.8_spmd.clone, body=%wide.region_5.7_spmd.clone.sunk | while | flops 208436736 | bytes 28954320 | solution.py:194
  125.0 7.3 broadcast_in_dim.222
  132.3 34.1 %slice_reduce_fusion.6 = f32[786432]{0:T(1024)} fusion(f32[1,786944]{1,0:T(1,128)S(1)} %broadcast_in_dim.222), kind=kLoop, calls=%fused_computation.4.clone.1 | loop fusion | bytes 6291456 | tf_op jit(solution)/shard_map/while/body/eval_jaxpr/while/body/eval_jaxpr/slice | solution.py:56
  181.1 7.8 broadcast_in_dim.222
  189.0 34.1 %slice_reduce_fusion.6 = f32[786432]{0:T(1024)} fusion(f32[1,786944]{1,0:T(1,128)S(1)} %broadcast_in_dim.222), kind=kLoop, calls=%fused_computation.4.clone.1 | loop fusion | bytes 6291456 | tf_op jit(solution)/shard_map/while/body/eval_jaxpr/while/body/eval_jaxpr/slice | solution.py:56
  237.9 7.3 broadcast_in_dim.222
  245.1 34.1 %slice_reduce_fusion.6 = f32[786432]{0:T(1024)} fusion(f32[1,786944]{1,0:T(1,128)S(1)} %broadcast_in_dim.222), kind=kLoop, calls=%fused_computation.4.clone.1 | loop fusion | bytes 6291456 | tf_op jit(solution)/shard_map/while/body/eval_jaxpr/while/body/eval_jaxpr/slice | solution.py:56
  294.0 7.3 broadcast_in_dim.222
  301.2 34.1 %slice_reduce_fusion.6 = f32[786432]{0:T(1024)} fusion(f32[1,786944]{1,0:T(1,128)S(1)} %broadcast_in_dim.222), kind=kLoop, calls=%fused_computation.4.clone.1 | loop fusion | bytes 6291456 | tf_op jit(solution)/shard_map/while/body/eval_jaxpr/while/body/eval_jaxpr/slice | solution.py:56
  350.1 7.3 broadcast_in_dim.222
  357.4 34.1 %slice_reduce_fusion.6 = f32[786432]{0:T(1024)} fusion(f32[1,786944]{1,0:T(1,128)S(1)} %broadcast_in_dim.222), kind=kLoop, calls=%fused_computation.4.clone.1 | loop fusion | bytes 6291456 | tf_op jit(solution)/shard_map/while/body/eval_jaxpr/while/body/eval_jaxpr/slice | solution.py:56
  406.2 7.3 broadcast_in_dim.222
  413.5 34.1 %slice_reduce_fusion.6 = f32[786432]{0:T(1024)} fusion(f32[1,786944]{1,0:T(1,128)S(1)} %broadcast_in_dim.222), kind=kLoop, calls=%fused_computation.4.clone.1 | loop fusion | bytes 6291456 | tf_op jit(solution)/shard_map/while/body/eval_jaxpr/while/body/eval_jaxpr/slice | solution.py:56
  462.3 7.3 broadcast_in_dim.222
  469.6 34.1 %slice_reduce_fusion.6 = f32[786432]{0:T(1024)} fusion(f32[1,786944]{1,0:T(1,128)S(1)} %broadcast_in_dim.222), kind=kLoop, calls=%fused_computation.4.clone.1 | loop fusion | bytes 6291456 | tf_op jit(solution)/shard_map/while/body/eval_jaxpr/while/body/eval_jaxpr/slice | solution.py:56
  518.4 7.3 broadcast_in_dim.222
  525.7 34.1 %slice_reduce_fusion.6 = f32[786432]{0:T(1024)} fusion(f32[1,786944]{1,0:T(1,128)S(1)} %broadcast_in_dim.222), kind=kLoop, calls=%fused_computation.4.clone.1 | loop fusion | bytes 6291456 | tf_op jit(solution)/shard_map/while/body/eval_jaxpr/while/body/eval_jaxpr/slice | solution.py:56
  574.5 7.3 broadcast_in_dim.222
  581.8 34.1 %slice_reduce_fusion.6 = f32[786432]{0:T(1024)} fusion(f32[1,786944]{1,0:T(1,128)S(1)} %broadcast_in_dim.222), kind=kLoop, calls=%fused_computation.4.clone.1 | loop fusion | bytes 6291456 | tf_op jit(solution)/shard_map/while/body/eval_jaxpr/while/body/eval_jaxpr/slice | solution.py:56
  630.6 7.3 broadcast_in_dim.222
  637.9 34.1 %slice_reduce_fusion.6 = f32[786432]{0:T(1024)} fusion(f32[1,786944]{1,0:T(1,128)S(1)} %broadcast_in_dim.222), kind=kLoop, calls=%fused_computation.4.clone.1 | loop fusion | bytes 6291456 | tf_op jit(solution)/shard_map/while/body/eval_jaxpr/while/body/eval_jaxpr/slice | solution.py:56
  686.7 7.3 broadcast_in_dim.222
  694.0 34.1 %slice_reduce_fusion.6 = f32[786432]{0:T(1024)} fusion(f32[1,786944]{1,0:T(1,128)S(1)} %broadcast_in_dim.222), kind=kLoop, calls=%fused_computation.4.clone.1 | loop fusion | bytes 6291456 | tf_op jit(solution)/shard_map/while/body/eval_jaxpr/while/body/eval_jaxpr/slice | solution.py:56
  742.8 7.3 broadcast_in_dim.222
  750.1 34.1 %slice_reduce_fusion.6 = f32[786432]{0:T(1024)} fusion(f32[1,786944]{1,0:T(1,128)S(1)} %broadcast_in_dim.222), kind=kLoop, calls=%fused_computation.4.clone.1 | loop fusion | bytes 6291456 | tf_op jit(solution)/shard_map/while/body/eval_jaxpr/while/body/eval_jaxpr/slice | solution.py:56
  797.9 19.8 multiply_convert_fusion.1
  828.0 9.2 convert_reduce_fusion
  847.5 1403.0 %while.57 = (s32[]{:T(128)}, f32[12,512,64]{1,2,0:T(8,128)}, f32[12,1536,64]{1,2,0:T(8,128)}, f32[12,1536,64]{1,2,0:T(8,128)}, f32[12,1024]{1,0:T(8,128)}, /*ind...) while((s32[]{:T(128)}, f32[12,512,64]{1,2,0:T(8,128)}, ...), condition=%wide.region_19.20_spmd.clone, body=%wide.region_16.19_spmd.clone.sunk | while | flops 518193152 | bytes 83129144 | solution.py:304
  859.4 7.3 broadcast_in_dim.226
  866.7 34.1 %slice_reduce_fusion.7 = f32[786432]{0:T(1024)} fusion(f32[1,786944]{1,0:T(1,128)S(1)} %broadcast_in_dim.226), kind=kLoop, calls=%fused_computation.29.clone.1 | loop fusion | bytes 6291456 | tf_op jit(solution)/shard_map/while/body/eval_jaxpr/while/body/eval_jaxpr/slice | solution.py:56
  922.7 32.5 %pad_reduce_fusion.8 = f32[786944]{0:T(1024)S(1)} fusion(f32[1,786432]{1,0:T(1,128)S(1)} %bitcast.247), kind=kLoop, calls=%fused_computation.27.clone.1 | loop fusion | bytes 6293504 | tf_op jit(solution)/shard_map/while/body/eval_jaxpr/while/body/eval_jaxpr/jit(_pad)/pad | solution.py:61
  982.4 34.1 %slice_reduce_fusion.7 = f32[786432]{0:T(1024)} fusion(f32[1,786944]{1,0:T(1,128)S(1)} %broadcast_in_dim.226), kind=kLoop, calls=%fused_computation.29.clone.1 | loop fusion | bytes 6291456 | tf_op jit(solution)/shard_map/while/body/eval_jaxpr/while/body/eval_jaxpr/slice | solution.py:56
  1038.4 32.5 %pad_reduce_fusion.8 = f32[786944]{0:T(1024)S(1)} fusion(f32[1,786432]{1,0:T(1,128)S(1)} %bitcast.247), kind=kLoop, calls=%fused_computation.27.clone.1 | loop fusion | bytes 6293504 | tf_op jit(solution)/shard_map/while/body/eval_jaxpr/while/body/eval_jaxpr/jit(_pad)/pad | solution.py:61
  1098.1 34.1 %slice_reduce_fusion.7 = f32[786432]{0:T(1024)} fusion(f32[1,786944]{1,0:T(1,128)S(1)} %broadcast_in_dim.226), kind=kLoop, calls=%fused_computation.29.clone.1 | loop fusion | bytes 6291456 | tf_op jit(solution)/shard_map/while/body/eval_jaxpr/while/body/eval_jaxpr/slice | solution.py:56
  1154.1 32.5 %pad_reduce_fusion.8 = f32[786944]{0:T(1024)S(1)} fusion(f32[1,786432]{1,0:T(1,128)S(1)} %bitcast.247), kind=kLoop, calls=%fused_computation.27.clone.1 | loop fusion | bytes 6293504 | tf_op jit(solution)/shard_map/while/body/eval_jaxpr/while/body/eval_jaxpr/jit(_pad)/pad | solution.py:61
  1213.9 34.1 %slice_reduce_fusion.7 = f32[786432]{0:T(1024)} fusion(f32[1,786944]{1,0:T(1,128)S(1)} %broadcast_in_dim.226), kind=kLoop, calls=%fused_computation.29.clone.1 | loop fusion | bytes 6291456 | tf_op jit(solution)/shard_map/while/body/eval_jaxpr/while/body/eval_jaxpr/slice | solution.py:56
  1269.9 32.5 %pad_reduce_fusion.8 = f32[786944]{0:T(1024)S(1)} fusion(f32[1,786432]{1,0:T(1,128)S(1)} %bitcast.247), kind=kLoop, calls=%fused_computation.27.clone.1 | loop fusion | bytes 6293504 | tf_op jit(solution)/shard_map/while/body/eval_jaxpr/while/body/eval_jaxpr/jit(_pad)/pad | solution.py:61
  1329.6 34.1 %slice_reduce_fusion.7 = f32[786432]{0:T(1024)} fusion(f32[1,786944]{1,0:T(1,128)S(1)} %broadcast_in_dim.226), kind=kLoop, calls=%fused_computation.29.clone.1 | loop fusion | bytes 6291456 | tf_op jit(solution)/shard_map/while/body/eval_jaxpr/while/body/eval_jaxpr/slice | solution.py:56
  1385.6 32.5 %pad_reduce_fusion.8 = f32[786944]{0:T(1024)S(1)} fusion(f32[1,786432]{1,0:T(1,128)S(1)} %bitcast.247), kind=kLoop, calls=%fused_computation.27.clone.1 | loop fusion | bytes 6293504 | tf_op jit(solution)/shard_map/while/body/eval_jaxpr/while/body/eval_jaxpr/jit(_pad)/pad | solution.py:61
  1445.3 34.1 %slice_reduce_fusion.7 = f32[786432]{0:T(1024)} fusion(f32[1,786944]{1,0:T(1,128)S(1)} %broadcast_in_dim.226), kind=kLoop, calls=%fused_computation.29.clone.1 | loop fusion | bytes 6291456 | tf_op jit(solution)/shard_map/while/body/eval_jaxpr/while/body/eval_jaxpr/slice | solution.py:56
  1501.3 32.5 %pad_reduce_fusion.8 = f32[786944]{0:T(1024)S(1)} fusion(f32[1,786432]{1,0:T(1,128)S(1)} %bitcast.247), kind=kLoop, calls=%fused_computation.27.clone.1 | loop fusion | bytes 6293504 | tf_op jit(solution)/shard_map/while/body/eval_jaxpr/while/body/eval_jaxpr/jit(_pad)/pad | solution.py:61
  1561.0 34.1 %slice_reduce_fusion.7 = f32[786432]{0:T(1024)} fusion(f32[1,786944]{1,0:T(1,128)S(1)} %broadcast_in_dim.226), kind=kLoop, calls=%fused_computation.29.clone.1 | loop fusion | bytes 6291456 | tf_op jit(solution)/shard_map/while/body/eval_jaxpr/while/body/eval_jaxpr/slice | solution.py:56
  1617.0 32.5 %pad_reduce_fusion.8 = f32[786944]{0:T(1024)S(1)} fusion(f32[1,786432]{1,0:T(1,128)S(1)} %bitcast.247), kind=kLoop, calls=%fused_computation.27.clone.1 | loop fusion | bytes 6293504 | tf_op jit(solution)/shard_map/while/body/eval_jaxpr/while/body/eval_jaxpr/jit(_pad)/pad | solution.py:61
  1676.8 34.1 %slice_reduce_fusion.7 = f32[786432]{0:T(1024)} fusion(f32[1,786944]{1,0:T(1,128)S(1)} %broadcast_in_dim.226), kind=kLoop, calls=%fused_computation.29.clone.1 | loop fusion | bytes 6291456 | tf_op jit(solution)/shard_map/while/body/eval_jaxpr/while/body/eval_jaxpr/slice | solution.py:56
  1732.8 32.5 %pad_reduce_fusion.8 = f32[786944]{0:T(1024)S(1)} fusion(f32[1,786432]{1,0:T(1,128)S(1)} %bitcast.247), kind=kLoop, calls=%fused_computation.27.clone.1 | loop fusion | bytes 6293504 | tf_op jit(solution)/shard_map/while/body/eval_jaxpr/while/body/eval_jaxpr/jit(_pad)/pad | solution.py:61
  1792.5 34.1 %slice_reduce_fusion.7 = f32[786432]{0:T(1024)} fusion(f32[1,786944]{1,0:T(1,128)S(1)} %broadcast_in_dim.226), kind=kLoop, calls=%fused_computation.29.clone.1 | loop fusion | bytes 6291456 | tf_op jit(solution)/shard_map/while/body/eval_jaxpr/while/body/eval_jaxpr/slice | solution.py:56
  1848.5 32.5 %pad_reduce_fusion.8 = f32[786944]{0:T(1024)S(1)} fusion(f32[1,786432]{1,0:T(1,128)S(1)} %bitcast.247), kind=kLoop, calls=%fused_computation.27.clone.1 | loop fusion | bytes 6293504 | tf_op jit(solution)/shard_map/while/body/eval_jaxpr/while/body/eval_jaxpr/jit(_pad)/pad | solution.py:61
  1908.2 34.1 %slice_reduce_fusion.7 = f32[786432]{0:T(1024)} fusion(f32[1,786944]{1,0:T(1,128)S(1)} %broadcast_in_dim.226), kind=kLoop, calls=%fused_computation.29.clone.1 | loop fusion | bytes 6291456 | tf_op jit(solution)/shard_map/while/body/eval_jaxpr/while/body/eval_jaxpr/slice | solution.py:56
  1964.2 32.5 %pad_reduce_fusion.8 = f32[786944]{0:T(1024)S(1)} fusion(f32[1,786432]{1,0:T(1,128)S(1)} %bitcast.247), kind=kLoop, calls=%fused_computation.27.clone.1 | loop fusion | bytes 6293504 | tf_op jit(solution)/shard_map/while/body/eval_jaxpr/while/body/eval_jaxpr/jit(_pad)/pad | solution.py:61
  2023.9 34.1 %slice_reduce_fusion.7 = f32[786432]{0:T(1024)} fusion(f32[1,786944]{1,0:T(1,128)S(1)} %broadcast_in_dim.226), kind=kLoop, calls=%fused_computation.29.clone.1 | loop fusion | bytes 6291456 | tf_op jit(solution)/shard_map/while/body/eval_jaxpr/while/body/eval_jaxpr/slice | solution.py:56
  2079.9 32.5 %pad_reduce_fusion.8 = f32[786944]{0:T(1024)S(1)} fusion(f32[1,786432]{1,0:T(1,128)S(1)} %bitcast.247), kind=kLoop, calls=%fused_computation.27.clone.1 | loop fusion | bytes 6293504 | tf_op jit(solution)/shard_map/while/body/eval_jaxpr/while/body/eval_jaxpr/jit(_pad)/pad | solution.py:61
  2139.7 34.1 %slice_reduce_fusion.7 = f32[786432]{0:T(1024)} fusion(f32[1,786944]{1,0:T(1,128)S(1)} %broadcast_in_dim.226), kind=kLoop, calls=%fused_computation.29.clone.1 | loop fusion | bytes 6291456 | tf_op jit(solution)/shard_map/while/body/eval_jaxpr/while/body/eval_jaxpr/slice | solution.py:56
  2195.7 32.5 %pad_reduce_fusion.8 = f32[786944]{0:T(1024)S(1)} fusion(f32[1,786432]{1,0:T(1,128)S(1)} %bitcast.247), kind=kLoop, calls=%fused_computation.27.clone.1 | loop fusion | bytes 6293504 | tf_op jit(solution)/shard_map/while/body/eval_jaxpr/while/body/eval_jaxpr/jit(_pad)/pad | solution.py:61
  2256.0 26.9 collective-permute-start.2
  2311.7 8.1 copy.90
  2321.2 7.4 fusion.99
  2329.7 8.1 fusion.119
  2345.0 105.6 %all-reduce.23.cloned.1.call-done = (f32[12,1024]{1,0:T(8,128)}, f32[2304]{0:T(1024)}, f32[768]{0:T(1024)}, f32[768]{0:T(1024)}, f32[768]{0:T(1024)}, /*index=5*...) async-done(((f32[12,1024]{1,0:T(8,128)}, f32[2304]{0:T(1024)}, f32[768]{0:T(1024)}, f32[768]{0:T(1024)}, f32[768]{0:T(1024)}, /*index=5*/f32[3072]{0:T(1024)}, ...) | async-done | bytes 89104 | tf_op jit(solution)/shard_map/psum | solution.py:342
  2460.6 96.0 %reduce-scatter.7.cloned.1.call-done = f32[24,768]{1,0:T(8,128)} async-done(((f32[768,768]{1,0:T(8,128)}), f32[24,768]{1,0:T(8,128)}) %reduce-scatter.7.cloned.1.call-update) | async-done | bytes 73744 | tf_op jit(solution)/shard_map/reduce_scatter | solution.py:346
  2556.6 124.4 %reduce-scatter.13.cloned.1.call-done = f32[24,2304]{1,0:T(8,128)} async-done(((f32[768,2304]{1,0:T(8,128)}), f32[24,2304]{1,0:T(8,128)}) %reduce-scatter.13.cloned.1.call-update) | async-done | bytes 221200
  2681.1 142.2 %reduce-scatter.9.cloned.1.call-done = f32[24,3072]{1,0:T(8,128)} async-done(((f32[768,3072]{1,0:T(8,128)}), f32[24,3072]{1,0:T(8,128)}) %reduce-scatter.9.cloned.1.call-update) | async-done | bytes 294928 | tf_op jit(solution)/shard_map/reduce_scatter | solution.py:350
  2823.2 141.1 %reduce-scatter.11.cloned.1.call-done = f32[96,768]{1,0:T(8,128)} async-done(((f32[3072,768]{1,0:T(8,128)}), f32[96,768]{1,0:T(8,128)}) %reduce-scatter.11.cloned.1.call-update) | async-done | bytes 294928 | tf_op jit(solution)/shard_map/reduce_scatter | solution.py:352
  (658 shorter events, 847.0 us)
Async XLA Ops:
  7.2 76.1 %copy-start = (f32[12,64,64]{2,1,0:T(8,128)S(1)}, f32[12,64,64]{2,1,0:T(8,128)}, u32[]{:S(2)}) copy-start(f32[12,64,64]{2,1,0:T(8,128)} %param.26) | copy-start | bytes 589828
  7.2 66.6 %all-gather.5.cloned.1.call-start = ((), (), s32[]{:S(2)}) async-start(), calls=%async_computation.4 | async-start | bytes 3649536 | tf_op jit(solution)/shard_map/all_gather | solution.py:120
  7.9 786.8 %all-gather.7.cloned.1.call-start = ((), (), s32[]{:S(2)}) async-start(), calls=%async_computation.5 | async-start | bytes 1216512 | tf_op jit(solution)/shard_map/all_gather | solution.py:122
  8.7 789.2 %all-gather.9.cloned.1.call-start = ((), (), s32[]{:S(2)}) async-start(), calls=%async_computation.6 | async-start | bytes 4866048 | tf_op jit(solution)/shard_map/all_gather | solution.py:126
  9.4 808.3 %all-gather.11.cloned.1.call-start = ((), (), s32[]{:S(2)}) async-start(), calls=%async_computation.7 | async-start | bytes 4866048 | tf_op jit(solution)/shard_map/all_gather | solution.py:128
  10.0 2440.5 %all-reduce.23.cloned.1.call-start = ((), (), s32[]{:S(2)}) async-start(), calls=%async_computation.12 | async-start | bytes 229376 | tf_op jit(solution)/shard_map/psum | solution.py:342
  87.7 6.4 copy-start.40
  87.7 7.0 copy-start.56
  87.8 7.1 copy-start.30
  87.8 7.8 copy-start.52
  87.8 8.4 copy-start.51
  87.8 9.0 copy-start.50
  87.8 10.1 copy-start.49
  87.8 10.7 copy-start.48
  87.8 10.7 copy-start.47
  89.3 16.4 collective-permute-start
  92.7 13.1 collective-permute-start.1
  797.5 43.5 %copy-start.10 = (f32[512,768]{1,0:T(8,128)}, f32[512,768]{1,0:T(8,128)S(1)}, u32[]{:S(2)}) copy-start(f32[512,768]{1,0:T(8,128)S(1)} %get-tuple-element.710) | copy-start | bytes 4718596
  797.5 43.5 %copy-start.31 = (f32[512]{0:T(512)}, f32[512]{0:T(512)S(1)}, u32[]{:S(2)}) copy-start(f32[512]{0:T(512)S(1)} %broadcast_multiply_fusion.4) | copy-start | bytes 6148
  797.8 43.2 %copy-start.38 = (f32[512]{0:T(512)}, f32[512]{0:T(512)S(1)}, u32[]{:S(2)}) copy-start(f32[512]{0:T(512)S(1)} %fusion.95) | copy-start | bytes 6148
  797.8 19.9 copy-start.45
  817.7 6.4 copy-start.6
  827.1 10.2 slice-start.2
  827.8 9.4 copy-start.25
  828.0 9.2 slice-start.3
  837.3 3.7 copy-start.57
  841.6 4.0 copy-start.13
  841.7 3.9 copy-start.41
  961.1 6.8 copy-start.1
  962.7 5.3 copy-start.2
  1076.8 6.9 copy-start.1
  1078.4 5.3 copy-start.2
  1192.6 6.8 copy-start.1
  1194.1 5.3 copy-start.2
  1308.3 6.9 copy-start.1
  1309.9 5.3 copy-start.2
  1424.0 6.8 copy-start.1
  1425.6 5.3 copy-start.2
  1539.8 6.8 copy-start.1
  1541.3 5.3 copy-start.2
  1655.5 6.8 copy-start.1
  1657.0 5.3 copy-start.2
  1771.2 6.8 copy-start.1
  1772.8 5.3 copy-start.2
  1886.9 6.8 copy-start.1
  1888.5 5.3 copy-start.2
  2002.7 6.8 copy-start.1
  2004.2 5.3 copy-start.2
  2118.4 6.9 copy-start.1
  2119.9 5.3 copy-start.2
  2234.1 6.8 copy-start.1
  2235.7 5.3 copy-start.2
  2250.6 3.7 slice-start.1
  2256.0 29.6 copy-start.7
  2256.0 30.3 %copy-start.9 = (f32[512,768]{1,0:T(8,128)S(1)}, f32[512,768]{1,0:T(8,128)}, u32[]{:S(2)}) copy-start(f32[512,768]{1,0:T(8,128)} %get-tuple-element.688) | copy-start | bytes 4718596
  2256.0 39.4 %collective-permute-start.2 = (bf16[512,1536]{0,1:T(8,128)(2,1)}, bf16[512,1536]{0,1:T(8,128)(2,1)}, u32[]{:S(2)}, u32[]{:S(2)}) collective-permute-start(bf16[512,1536]{0,1:T(8,128)(2,1)} %pad_maximum_fusion.3), channel_id=1, source_target_pairs={{0,2},{2,4},{4,6},{6,8},{8,10},{10,12},{12,14},{14,16},{16,18},{18... | collective-permute-start | bytes 4718600 | tf_op jit(solution)/shard_map/ppermute | solution.py:32
  2284.1 3.8 copy-start.8
  2284.1 11.2 collective-permute-start.3
  2295.3 6.1 copy-start.21
  2298.8 6.6 copy-start.15
  2302.5 254.1 %reduce-scatter.7.cloned.1.call-start = ((), (), s32[]{:S(2)}) async-start(), calls=%async_computation.8 | async-start | bytes 2433024 | tf_op jit(solution)/shard_map/reduce_scatter | solution.py:346
  2305.4 375.7 %reduce-scatter.13.cloned.1.call-start = ((), (), s32[]{:S(2)}) async-start(), calls=%async_computation.11 | async-start | bytes 7299072
  2319.8 503.4 %reduce-scatter.9.cloned.1.call-start = ((), (), s32[]{:S(2)}) async-start(), calls=%async_computation.9 | async-start | bytes 9732096 | tf_op jit(solution)/shard_map/reduce_scatter | solution.py:350
  2328.6 635.7 %reduce-scatter.11.cloned.1.call-start = ((), (), s32[]{:S(2)}) async-start(), calls=%async_computation.10 | async-start | bytes 9732096 | tf_op jit(solution)/shard_map/reduce_scatter | solution.py:352
  (33 other events, 67.0 us)
Sparse Core Ops, SparseCore 0:
  10.9 62.8 all-gather.4
  76.8 59.6 all-gather.6
  139.4 62.5 all-gather.8
  204.7 62.4 all-gather.10
  2302.6 147.8 all-reduce.22
  2457.1 99.5 reduce-scatter.6
  2562.9 118.1 reduce-scatter.12
  2688.6 134.6 reduce-scatter.8
  2829.7 134.5 reduce-scatter.10
where the time goes:
time: 2990 us; the launch traced here: 2970 us
  local copies, waits for them, and re-layouts  1790 us (60%)
  waiting for transfers between devices  625 us (21%)
  matrix products  325 us (11%)
  other arithmetic  77.6 us (3%)
  loops' own time  61.9 us (2%)
  blocking collectives  43 us (1%)
  starting transfers between devices  33.4 us (1%)
    slice x24, local copies, waits for them, and re-layouts, toeplitz(): return tiled[:, :q_block * key_span].reshape(head_count, q_block, key_span)  819 us
    pad x12, local copies, waits for them, and re-layouts, diagonal_sums(): jnp.pad(matrix.reshape(head_count, q_block * key_span), ((0, 0), (0, q_bl...  390 us
    broadcast_in_dim x48, local copies, waits for them, and re-layouts, toeplitz(): jnp.broadcast_to(padded[:, None, :], (head_count, q_block, key_span + 1))  221 us
    reduce_scatter x1, waiting for transfers between devices, on_device(): lax.psum_scatter(grad_up_w, ('seq', 'row'), scatter_dimension=0, tiled=True)  142 us
    reduce_scatter x1, waiting for transfers between devices, on_device(): lax.psum_scatter(grad_down_w, ('seq', 'row'), scatter_dimension=0, tiled=...  141 us
    unnamed x10, waiting for transfers between devices  127 us
    psum x1, waiting for transfers between devices, on_device(): grad_rel = lax.psum(grad_bias, ('seq', 'row'))  106 us
    reduce_scatter x1, waiting for transfers between devices, on_device(): lax.psum_scatter(grad_out_w, ('seq', 'row'), scatter_dimension=0, tiled=T...  96 us
  transfers between devices with their start and end apart: 13, of which 6 were waited for; matrix products, arithmetic and copies ran while one was open for 26% of the time, Pallas kernels for 0%

commit v1 on v0

--- a/solution.py
+++ b/solution.py
@@ -1,9 +1,177 @@
 from functools import partial
 
+import functools
 import jax
 import jax.numpy as jnp
 from jax import lax
+from jax.experimental import pallas as pl
+from jax.experimental.pallas import tpu as pltpu
 from jax.sharding import PartitionSpec as P
+
+F32, BF16 = jnp.float32, jnp.bfloat16
+NT = (((1,), (1,)), ((), ()))
+TN = (((0,), (0,)), ((), ()))
+SB = 128
+
+def dot(a, b, dims=None):
+    if dims is None:
+        return jnp.dot(a, b, preferred_element_type=F32)
+    return lax.dot_general(a, b, dims, preferred_element_type=F32)
+
+def toep(row, width):
+    win = row.shape[1]
+    wide = jnp.concatenate([row, jnp.zeros((1, width - win), F32)], 1)
+    return pltpu.roll(jnp.broadcast_to(wide, (SB, width)), 0, 1, stride=1, stride_axis=0)
+
+def unskew(p, win):
+    rows = p.shape[0]; width = p.shape[1]
+    while rows > 8:
+        rows //= 2
+        p = p[:rows] + pltpu.roll(p[rows:], width - rows, 1)
+    r = lax.broadcasted_iota(jnp.int32, (8, 1), 0)
+    for s in (1, 2, 4):
+        p = jnp.where((r & s) != 0, pltpu.roll(p, width - s, 1), p)
+    return jnp.sum(p, 0, keepdims=True)[:, :win]
+
+def fill_mask(mask_s, dq_ref, dk_ref, pk_ref, span, half):
+    S = mask_s.shape[0]
+    for a in range(S // SB):
+        dq = dq_ref[a*SB:(a+1)*SB, :]
+        dk = dk_ref[:, a*SB:a*SB+span]
+        pk = pk_ref[:, a*SB:a*SB+span]
+        r = lax.broadcasted_iota(jnp.int32, (SB, span), 0)
+        c = lax.broadcasted_iota(jnp.int32, (SB, span), 1)
+        ok = (dq == dk) & ((pk == 1) | (c == r + half))
+        mask_s[a*SB:(a+1)*SB, :] = jnp.where(ok, 1.0, 0.0)
+
+def halves(x):
+    lane = lax.broadcasted_iota(jnp.int32, x.shape, 1)
+    z = jnp.zeros_like(x)
+    return jnp.where(lane < 64, x, z), jnp.where(lane >= 64, x, z)
+
+def pick(a, b):
+    lane = lax.broadcasted_iota(jnp.int32, a.shape, 1)
+    return jnp.where(lane < 64, a, b)
+
+def fwd_kernel(CH, dq_ref, dk_ref, pk_ref, bias_ref, q_ref, k_ref, v_ref, att_ref, inv_ref, mask_s, t_s, w_s, v_s):
+    S = q_ref.shape[0]; win = bias_ref.shape[1]; span = win + SB
+    p = pl.program_id(0)
+    @pl.when(p == 0)
+    def _():
+        fill_mask(mask_s, dq_ref, dk_ref, pk_ref, span, win // 2)
+        v_s[:, 128:] = jnp.ones((v_s.shape[0], 128), BF16)
+    rows = jnp.exp(bias_ref[pl.ds(pl.multiple_of(p * 8, 8), 8), :])
+    for i in range(2):
+        t_s[i*SB:(i+1)*SB, :] = toep(rows[i:i+1], span)
+    v_s[:, :128] = v_ref[...]
+    for a in range(S // SB):
+        qa, qb = halves(q_ref[a*SB:(a+1)*SB, :])
+        qq = jnp.concatenate([qa, qb], 0)
+        for c in range(0, span, CH):
+            s = dot(qq, k_ref[a*SB+c:a*SB+c+CH, :], NT)
+            m = mask_s[a*SB:(a+1)*SB, c:c+CH]
+            t = t_s[:, c:c+CH]
+            w_s[:SB, c:c+CH] = (s[:SB] * (t[:SB] * m)).astype(BF16)
+            w_s[SB:, c:c+CH] = (s[SB:] * (t[SB:] * m)).astype(BF16)
+        o = dot(w_s[...], v_s[a*SB:a*SB+span, :])
+        inv = 1.0 / pick(o[:SB, 128:], o[SB:, 128:])
+        att_ref[a*SB:(a+1)*SB, :] = pick(o[:SB, :128], o[SB:, :128]) * inv
+        inv_ref[a*SB:(a+1)*SB, :] = inv
+
+def bias_rows(rel_bias):
+    h, w = rel_bias.shape
+    x = rel_bias.reshape(h // 2, 2, w)
+    return jnp.pad(x, ((0, 0), (0, 6), (0, 0))).reshape(h // 2 * 8, w)
+
+def attn_fwd(dq, dk, pk, bias8, q, k, v, CH=384):
+    S, D = q.shape; KS = k.shape[0]; win = bias8.shape[1]; span = win + SB
+    full = lambda *s: pl.BlockSpec(s, lambda p: (0,) * len(s))
+    col = lambda n: pl.BlockSpec((n, 128), lambda p: (0, p))
+    return pl.pallas_call(
+        functools.partial(fwd_kernel, CH),
+        grid=(D // 128,),
+        out_shape=(jax.ShapeDtypeStruct((S, D), F32), jax.ShapeDtypeStruct((S, D), F32)),
+        in_specs=[full(S, 1), full(1, KS), full(1, KS), full(*bias8.shape), col(S), col(KS), col(KS)],
+        out_specs=(col(S), col(S)),
+        scratch_shapes=[pltpu.VMEM((S, span), F32), pltpu.VMEM((2*SB, span), F32), pltpu.VMEM((2*SB, span), BF16), pltpu.VMEM((KS, 256), BF16)],
+        compiler_params=pltpu.CompilerParams(vmem_limit_bytes=48 << 20),
+        name="attn_fwd",
+    )(dq, dk, pk, bias8, q, k, v)
+
+def bwd_kernel(CH, dq_ref, dk_ref, pk_ref, bias_ref, q_ref, k_ref, v_ref, att_ref, inv_ref, ga_ref,
+               gq_ref, gk_ref, gv_ref, gb_ref, mask_s, t_s, w_s, gs_s, p_s, v_s, gk_s, gv_s):
+    S = q_ref.shape[0]; win = bias_ref.shape[1]; span = win + SB
+    p = pl.program_id(0)
+    @pl.when(p == 0)
+    def _():
+        fill_mask(mask_s, dq_ref, dk_ref, pk_ref, span, win // 2)
+        v_s[:, 128:] = jnp.ones((v_s.shape[0], 128), BF16)
+    rows = jnp.exp(bias_ref[pl.ds(pl.multiple_of(p * 8, 8), 8), :])
+    for i in range(2):
+        t_s[i*SB:(i+1)*SB, :] = toep(rows[i:i+1], span)
+    v_s[:, :128] = v_ref[...]
+    gk_s[...] = jnp.zeros_like(gk_s)
+    gv_s[...] = jnp.zeros_like(gv_s)
+    for a in range(S // SB):
+        rs = slice(a*SB, (a+1)*SB)
+        qa, qb = halves(q_ref[rs, :])
+        qq = jnp.concatenate([qa, qb], 0)
+        ga = ga_ref[rs, :]
+        inv = inv_ref[rs, :]
+        gw = (ga * inv).astype(BF16)
+        gwa, gwb = halves(gw)
+        pr = ga * att_ref[rs, :] * inv
+        pa, pb = halves(pr)
+        lane = lax.broadcasted_iota(jnp.int32, (SB, 128), 1)
+        def ext(x):
+            g = -jnp.sum(x, 1, keepdims=True)
+            hi = g.astype(BF16)
+            lo = (g - hi.astype(F32)).astype(BF16)
+            z = jnp.zeros((SB, 128), BF16)
+            return jnp.where(lane == 0, hi, jnp.where(lane == 1, lo, z))
+        gg = jnp.concatenate([jnp.concatenate([gwa, ext(pa)], 1), jnp.concatenate([gwb, ext(pb)], 1)], 0)
+        for c in range(0, span, CH):
+            s = dot(qq, k_ref[a*SB+c:a*SB+c+CH, :], NT)
+            g = dot(gg, v_s[a*SB+c:a*SB+c+CH, :], NT)
+            m = mask_s[rs, c:c+CH]
+            for h in range(2):
+                hs = slice(h*SB, (h+1)*SB)
+                cm = t_s[hs, c:c+CH] * m
+                w = s[hs] * cm
+                w_s[hs, c:c+CH] = w.astype(BF16)
+                gs_s[hs, c:c+CH] = (g[hs] * cm).astype(BF16)
+                pw = g[hs] * w
+                if a == 0:
+                    p_s[hs, c:c+CH] = pw
+                else:
+                    p_s[hs, c:c+CH] += pw
+        gq = dot(gs_s[...], k_ref[a*SB:a*SB+span, :])
+        gq_ref[rs, :] = pick(gq[:SB], gq[SB:])
+        gk_s[:, a*SB:a*SB+span] += dot(qq, gs_s[...], TN)
+        gwq = jnp.concatenate([gwa, gwb], 0)
+        gv_s[:, a*SB:a*SB+span] += dot(gwq, w_s[...], TN)
+    gk_ref[...] = gk_s[...].T
+    gv_ref[...] = gv_s[...].T
+    gb_ref[...] = jnp.concatenate([unskew(p_s[:SB, :], win), unskew(p_s[SB:, :], win), jnp.zeros((6, win), F32)], 0)
+
+def attn_bwd(dq, dk, pk, bias8, q, k, v, att, inv, ga, CH=384):
+    S, D = q.shape; KS = k.shape[0]; win = bias8.shape[1]; span = win + SB
+    full = lambda *s: pl.BlockSpec(s, lambda p: (0,) * len(s))
+    col = lambda n: pl.BlockSpec((n, 128), lambda p: (0, p))
+    V = pltpu.VMEM
+    return pl.pallas_call(
+        functools.partial(bwd_kernel, CH),
+        grid=(D // 128,),
+        out_shape=(jax.ShapeDtypeStruct((S, D), F32), jax.ShapeDtypeStruct((KS, D), F32), jax.ShapeDtypeStruct((KS, D), F32),
+                   jax.ShapeDtypeStruct(bias8.shape, F32)),
+        in_specs=[full(S, 1), full(1, KS), full(1, KS), full(*bias8.shape), col(S), col(KS), col(KS), col(S), col(S), col(S)],
+        out_specs=(col(S), col(KS), col(KS), pl.BlockSpec((8, win), lambda p: (p, 0))),
+        scratch_shapes=[V((S, span), F32), V((2*SB, span), F32), V((2*SB, span), BF16), V((2*SB, span), BF16), V((2*SB, span), F32),
+                        V((KS, 256), BF16), V((128, KS), F32), V((128, KS), F32)],
+        compiler_params=pltpu.CompilerParams(vmem_limit_bytes=56 << 20),
+        name="attn_bwd",
+    )(dq, dk, pk, bias8, q, k, v, att, inv, ga)
+
 
 EPS = 1e-06
 EXACT_MATMUL = lax.Precision.HIGHEST
@@ -47,40 +215,10 @@
     return jnp.exp(projected_rows - half_square) * random_features.shape[1] ** (-0.5)
 
 
-def toeplitz(rows_in, q_block):
-    head_count, window_len = rows_in.shape
-    key_span = q_block + window_len
-    padded = jnp.pad(rows_in, ((0, 0), (0, key_span + 1 - window_len)))
-    tiled = jnp.broadcast_to(padded[:, None, :], (head_count, q_block, key_span + 1))
-    tiled = tiled.reshape(head_count, q_block * (key_span + 1))
-    return tiled[:, : q_block * key_span].reshape(head_count, q_block, key_span)
-
-
-def diagonal_sums(matrix, window_len):
-    head_count, q_block, key_span = matrix.shape
-    flat = jnp.pad(matrix.reshape(head_count, q_block * key_span), ((0, 0), (0, q_block)))
-    return jnp.sum(flat.reshape(head_count, q_block, key_span + 1)[:, :, :window_len], 1)
-
-
 def document_numbers(positions, lengths_row):
     ends = jnp.cumsum(lengths_row)
     counted = jnp.sum((positions[:, None] >= ends[None, :]).astype(jnp.int32), -1)
     return jnp.where(positions < 0, -1, counted)
-
-
-def band_mask(doc_query, doc_keys, pad_keys, half_win):
-    row_count = doc_query.shape[0]
-    col_count = doc_keys.shape[0]
-    diagonal = (
-        jnp.arange(col_count, dtype=jnp.int32)[None, :]
-        == jnp.arange(row_count, dtype=jnp.int32)[:, None] + half_win
-    )
-    same_doc = doc_query[:, None] == doc_keys[None, :]
-    return jnp.where(same_doc & ((pad_keys[None, :] == 1) | diagonal), 1.0, 0.0).astype(jnp.float32)
-
-
-def take_head(array, head):
-    return lax.dynamic_index_in_dim(array, head, 1, keepdims=False)
 
 
 def on_device(
@@ -112,10 +250,6 @@
     feat_count = feature_draws.shape[1]
     head_dim = model_width // head_count
     feat_cols = head_count * feat_count
-    q_block = min(512, seq_len)
-    block_count = seq_len // q_block
-    key_span = q_block + window_len
-    exp_bias = jnp.exp(rel_bias)
     params = (
         lax.all_gather(w_qkv, ("seq", "row"), axis=0, tiled=True),
         lax.all_gather(b_qkv, ("seq", "row"), axis=0, tiled=True),
@@ -166,36 +300,11 @@
     rims = padded_2(masked_keys, (("seq", 0),), half_win)
     key_ext = jnp.concatenate([rims[:half_win], own_keys, rims[half_win + seq_len :]], 0)
 
-    def window_of():
-        keys_w = key_ext[:, :feat_cols].reshape(key_span, head_count, feat_count)
-        values_w = key_ext[:, feat_cols:].reshape(key_span, head_count, head_dim)
-        mask = band_mask(doc_query, doc_keys, pad_keys, half_win)
-        return (q_feat, keys_w, values_w, mask)
-
-    def head_coef(head):
-        return toeplitz(lax.dynamic_slice_in_dim(exp_bias, head, 1, 0), q_block)[0]
-
-    def attend(start):
-        fq_blk, keys_w, values_w, mask = window_of()
-
-        def per_head(head):
-            fq_head = take_head(fq_blk, head)
-            keys_head = take_head(keys_w, head)
-            score = jnp.einsum("qm,km->qk", fq_head, keys_head, preferred_element_type=jnp.float32)
-            weight = score * head_coef(head) * mask
-            totals = jnp.sum(weight, -1)
-            weighted = jnp.dot(
-                weight.astype(jnp.bfloat16),
-                take_head(values_w, head),
-                preferred_element_type=jnp.float32,
-            )
-            return (weighted / totals[:, None], totals)
-
-        return lax.map(per_head, jnp.arange(head_count, dtype=jnp.int32))
-
-    starts = jnp.arange(block_count, dtype=jnp.int32) * q_block
-    att_heads, totals_all = lax.map(attend, starts)
-    attended = att_heads.transpose(0, 2, 1, 3).reshape(seq_len, model_width)
+    dq, dk, pk = doc_query[:, None], doc_keys[None, :], pad_keys[None, :]
+    bias8 = bias_rows(rel_bias)
+    q_low = q_feat.reshape(seq_len, feat_cols)
+    keys_x, vals_x = key_ext[:, :feat_cols], key_ext[:, feat_cols:]
+    attended, inv_tot = attn_fwd(dq, dk, pk, bias8, q_low, keys_x, vals_x)
     att_low = attended.astype(jnp.bfloat16)
     branch = jnp.dot(att_low, out_w, preferred_element_type=jnp.float32) + out_b
     resid_one = local.astype(jnp.float32) + branch
@@ -259,65 +368,10 @@
     grad_out_w = jnp.einsum("ti,tj->ij", att_low, grad_one_low, preferred_element_type=jnp.float32)
     grad_out_b = jnp.sum(grad_one_low, 0, dtype=jnp.float32)
     grad_att = jnp.dot(grad_one_low, out_w.T, preferred_element_type=jnp.float32)
-    grad_att_heads = grad_att.reshape(block_count, q_block, head_count, head_dim).transpose(
-        0, 2, 1, 3
-    )
-
-    def back_block(carry, inputs):
-        grad_kf, grad_vv, grad_bias = carry
-        start, grad_att_blk, att_blk, totals_blk = inputs
-        fq_blk, keys_w, values_w, mask = window_of()
-
-        def per_head_back(head):
-            fq_head = take_head(fq_blk, head)
-            keys_head = take_head(keys_w, head)
-            values_head = take_head(values_w, head)
-            coef_head = head_coef(head)
-            score = jnp.einsum("qm,km->qk", fq_head, keys_head, preferred_element_type=jnp.float32)
-            weight = score * coef_head * mask
-            inverse = 1.0 / totals_blk[head]
-            grad_head = grad_att_blk[head]
-            grad_weighted = (grad_head * inverse[:, None]).astype(jnp.bfloat16)
-            grad_total = -jnp.sum(grad_head * att_blk[head], -1) * inverse
-            grad_weight = (
-                jnp.einsum(
-                    "qd,kd->qk", grad_weighted, values_head, preferred_element_type=jnp.float32
-                )
-                + grad_total[:, None]
-            )
-            grad_score = (grad_weight * coef_head * mask).astype(jnp.bfloat16)
-            grad_fq = jnp.einsum(
-                "qk,km->qm", grad_score, keys_head, preferred_element_type=jnp.float32
-            )
-            grad_keys_head = jnp.einsum(
-                "qk,qm->km", grad_score, fq_head, preferred_element_type=jnp.float32
-            )
-            grad_values_head = jnp.einsum(
-                "qk,qd->kd",
-                weight.astype(jnp.bfloat16),
-                grad_weighted,
-                preferred_element_type=jnp.float32,
-            )
-            grad_bias_head = diagonal_sums((grad_weight * weight)[None], window_len)[0]
-            return (grad_fq, grad_keys_head, grad_values_head, grad_bias_head)
-
-        grad_fq_blk, key_part, value_part, bias_part = lax.map(
-            per_head_back, jnp.arange(head_count, dtype=jnp.int32)
-        )
-        key_part = key_part.transpose(1, 0, 2).reshape(key_span, feat_cols)
-        value_part = value_part.transpose(1, 0, 2).reshape(key_span, model_width)
-        grad_kf = grad_kf + key_part
-        grad_vv = grad_vv + value_part
-        return ((grad_kf, grad_vv, grad_bias + bias_part), grad_fq_blk.transpose(1, 0, 2))
-
-    carry_init = (
-        jnp.zeros((seq_len + window_len, feat_cols), jnp.float32),
-        jnp.zeros((seq_len + window_len, model_width), jnp.float32),
-        jnp.zeros((head_count, window_len), jnp.float32),
-    )
-    (grad_kf, grad_vv, grad_bias), grad_fq_all = lax.scan(
-        back_block, carry_init, (starts, grad_att_heads, att_heads, totals_all)
-    )
+    grad_fq_all, grad_kf, grad_vv, grad_b8 = attn_bwd(
+        dq, dk, pk, bias8, q_low, keys_x, vals_x, attended, inv_tot, grad_att
+    )
+    grad_bias = grad_b8.reshape(head_count // 2, 8, window_len)[:, :2].reshape(head_count, window_len)
     lower_rim = jnp.concatenate([grad_kf[:half_win], grad_vv[:half_win]], 1)
     upper_rim = jnp.concatenate([grad_kf[half_win + seq_len :], grad_vv[half_win + seq_len :]], 1)
     from_right = passed_along(lower_rim.astype(jnp.bfloat16), "seq", -1).astype(lower_rim.dtype)

time: 2990 us -> 1050 us (0.35)
  local copies, waits for them, and re-layouts: 1790 us -> 62.2 us
  matrix products: 325 us -> 90.4 us
  waiting for transfers between devices: 625 us -> 750 us
  loops' own time: 61.9 us -> 0 us
  other arithmetic: 77.6 us -> 31.9 us
  Pallas kernels: 0 us -> 39.9 us
    slice x29 -> x2, local copies, waits for them, and re-layouts: 831 us -> 3.4 us  [the longest x1 2.46 us: on_device(): keys_x, vals_x = (key_ext[:, :feat_cols], key_ext[:, feat_cols:])]
    pad x36 -> x0, local copies, waits for them, and re-layouts: 391 us -> none  [the longest x12 390 us: diagonal_sums(): jnp.pad(matrix.reshape(head_count, q_block * key_span), ((0, 0), (0, q_bl...]
    dot_general x84 -> x0, matrix products: 239 us -> none  [the longest x12 58 us: per_head_back(): jnp.einsum('qd,kd->qk', grad_weighted, values_head, preferred_element_typ...]
    broadcast_in_dim x48 -> x1, local copies, waits for them, and re-layouts: 221 us -> 0.01 us  [on_device(): dq, dk, pk = (doc_query[:, None], doc_keys[None, :], pad_keys[None, :])]
    reshape x36 -> x6, local copies, waits for them, and re-layouts: 118 us -> 6.9 us  [the longest x1 2.42 us: on_device(): grad_queries.reshape(seq_len, model_width)]
    dynamic_slice x84 -> x0, local copies, waits for them, and re-layouts: 110 us -> none  [the longest x24 41.1 us: per_head_back(): grad_total = -jnp.sum(grad_head * att_blk[head], -1) * inverse]
    another operation x2 -> x0, loops' own time: 61.9 us -> none  [the longest x1 38.1 us: back_block(): lax.map(per_head_back, jnp.arange(head_count, dtype=jnp.int32))]
    all_gather x1, waiting for transfers between devices: 0.02 us -> 61.7 us  [on_device(): lax.all_gather(w_up, ('seq', 'row'), axis=0, tiled=True)]
  transfers between devices with their start and end apart: 13 -> 13, of which waited for: 6 -> 9; matrix products, arithmetic and copies ran while one was open for 26% -> 11% of each run, Pallas kernels for 0% -> 1%
where the time goes in v1:
time: 1050 us; the launch traced here: 1040 us
  waiting for transfers between devices  750 us (71%)
  matrix products  90.4 us (9%)
  local copies, waits for them, and re-layouts  62.2 us (6%)
  blocking collectives  42.8 us (4%)
  Pallas kernels  39.9 us (4%)
  other arithmetic  31.9 us (3%)
  between operations  15 us (1%)
  starting transfers between devices  11.7 us (1%)
    reduce_scatter x1, waiting for transfers between devices, on_device(): lax.psum_scatter(grad_up_w, ('seq', 'row'), scatter_dimension=0, tiled=True)  142 us
    reduce_scatter x1, waiting for transfers between devices, on_device(): lax.psum_scatter(grad_down_w, ('seq', 'row'), scatter_dimension=0, tiled=...  141 us
    unnamed x10, waiting for transfers between devices  127 us
    psum x1, waiting for transfers between devices, on_device(): grad_rel = lax.psum(grad_bias, ('seq', 'row'))  110 us
    reduce_scatter x1, waiting for transfers between devices, on_device(): lax.psum_scatter(grad_out_w, ('seq', 'row'), scatter_dimension=0, tiled=T...  96 us
    all_gather x1, waiting for transfers between devices, on_device(): lax.all_gather(w_up, ('seq', 'row'), axis=0, tiled=True)  61.7 us
    all_gather x1, waiting for transfers between devices, on_device(): lax.all_gather(w_down, ('seq', 'row'), axis=0, tiled=True)  44.4 us
    unnamed x1, blocking collectives  42.8 us
  transfers between devices with their start and end apart: 13, of which 9 were waited for; matrix products, arithmetic and copies ran while one was open for 11% of the time, Pallas kernels for 1%

profile of v1, /device:TPU:0, one launch (start us, length us, event | category | flops | bytes accessed | tf_op | source)
XLA Modules:
  0.0 1044.1 jit_solution(18003979019557894131)
XLA Ops:
  16.8 42.8 %all-reduce.18 = (bf16[768]{0:T(1024)(128)(2,1)S(1)}, bf16[2304]{0:T(1024)(128)(2,1)S(1)}, bf16[768]{0:T(1024)(128)(2,1)S(1)}, bf16[768]{0:T(1024)(128)(2,1)S(1)...) all-reduce(bf16[768]{0:T(1024)(128)(2,1)S(1)} %dynamic-update-slice, ...), channel_id=1, replica_groups=mesh['seq'=16,'row'=2] {'seq','row'}, use_global_device_ids=true, to_apply=%add.2 | all-reduce | flops 9984 | bytes 39936
  61.2 12.7 %all-gather.5.cloned.1.call-done = bf16[768,2304]{1,0:T(8,128)(2,1)} async-done(((bf16[24,2304]{1,0:T(8,128)(2,1)}), bf16[768,2304]{1,0:T(8,128)(2,1)}) %all-gather.5.cloned.1.call-update) | async-done | bytes 3538960 | tf_op jit(solution)/shard_map/all_gather | solution.py:254
  74.0 4.2 convolution_add_fusion
  78.2 2.9 slice_add_fusion.2
  81.2 1.9 copy.80
  83.3 3.0 multiply_convert_fusion.1
  86.4 1.4 copy.81
  88.0 1.3 pad_maximum_fusion.2
  89.3 1.3 collective-permute-start.1
  90.6 4.2 collective-permute-start
  95.4 2.0 copy.79
  97.6 3.0 multiply_convert_fusion.2
  100.6 1.5 copy.83.q_ref
  102.1 3.4 pad_maximum_fusion
  105.6 2.5 fusion.48
  108.1 12.2 %attn_fwd.1 = (f32[512,768]{1,0:T(8,128)S(1)}, f32[512,768]{1,0:T(8,128)S(1)}) custom-call(s32[512,1]{1,0:T(8,128)S(1)} %fusion.38.dq_ref, s32[1,1536]{1,0:T(1,128)S(1)} %compare_select_fusion.dk_ref, s32[1,1536]{1,0:T(1,128)S(1)} %broadcast_in_dim.25.pk_ref, f32[48,1024]{1,0:T(8,128)S(1)} %pad_bitcast_fusion.bias_ref, bf16[512,768]{1,0:T(8,128)(2,1)S(1)} %copy.83.q_ref, ...), custom_call_target="tpu_custom_call" | custom-call | tf_op jit(solution)/shard_map/attn_fwd/pallas_call | solution.py:90
  121.4 15.0 %all-gather.7.cloned.1.call-done = bf16[768,768]{1,0:T(8,128)(2,1)} async-done(((bf16[24,768]{1,0:T(8,128)(2,1)}), bf16[768,768]{1,0:T(8,128)(2,1)}) %all-gather.7.cloned.1.call-update) | async-done | bytes 1179664 | tf_op jit(solution)/shard_map/all_gather | solution.py:256
  136.4 2.4 fusion.52
  140.2 61.7 %all-gather.9.cloned.1.call-done = bf16[768,3072]{1,0:T(8,128)(2,1)} async-done(((bf16[24,3072]{1,0:T(8,128)(2,1)}), bf16[768,3072]{1,0:T(8,128)(2,1)}) %all-gather.9.cloned.1.call-update) | async-done | bytes 4718608 | tf_op jit(solution)/shard_map/all_gather | solution.py:260
  201.9 20.9 %multiply_convert_fusion = (bf16[512,3072]{1,0:T(8,128)(2,1)}, f32[512,3072]{1,0:T(8,128)}, f32[512,3072]{1,0:T(8,128)}) fusion(f32[3072]{0:T(1024)S(1)} %convert_element_type.119, bf16[768,3072]{1,0:T(8,128)(2,1)} %all-gather.9.cloned.1.call-done, f32[512,768]{1,0:T(8,128)} %copy-done.16, f32[768]{0:T(1024)S(1)} %convert_element_type.117, ...), kind=kOutput, calls=%fused_computation.4 | convolution fusion | flops 2521694208 | bytes 22042624 | tf_op jit(solution)/shard_map/dot_general | solution.py:315
  222.8 44.4 %all-gather.11.cloned.1.call-done = bf16[3072,768]{1,0:T(8,128)(2,1)} async-done(((bf16[96,768]{1,0:T(8,128)(2,1)}), bf16[3072,768]{1,0:T(8,128)(2,1)}) %all-gather.11.cloned.1.call-update) | async-done | bytes 4718608 | tf_op jit(solution)/shard_map/all_gather | solution.py:262
  267.2 6.0 fusion.53
  274.4 1.3 fusion.11
  275.7 1.6 fusion.46
  278.3 10.0 convert_reduce_fusion
  288.3 5.7 multiply_reduce_fusion
  296.7 2.0 fusion.54.ga_ref
  298.7 27.7 %attn_bwd.1 = (f32[512,768]{1,0:T(8,128)}, f32[1536,768]{1,0:T(8,128)}, f32[1536,768]{1,0:T(8,128)}, f32[48,1024]{1,0:T(8,128)}) custom-call(s32[512,1]{1,0:T(8,128)} %copy-done.4, s32[1,1536]{1,0:T(1,128)} %copy-done.8, s32[1,1536]{1,0:T(1,128)} %copy-done.7, f32[48,1024]{1,0:T(8,128)} %copy-done.5, bf16[512,768]{1,0:T(8,128)(2,1)} %copy-done.1, ...), custom_call_target="tpu_custom_call" | custom-call | tf_op jit(solution)/shard_map/attn_bwd/pallas_call | solution.py:162
  326.4 2.7 convert.29
  330.5 1.3 pad_maximum_fusion.4
  331.7 1.3 collective-permute-start.3
  333.0 1.3 pad_maximum_fusion.3
  334.3 4.4 collective-permute-start.2
  339.4 1.6 copy.88
  341.1 1.7 copy.84
  344.4 2.4 convert_add_fusion
  346.8 4.1 fusion.14
  350.9 2.0 copy.89
  354.3 2.5 fusion.16
  356.9 2.3 copy.92
  359.2 2.0 copy.86
  362.6 2.5 fusion.20
  365.2 2.4 copy.91
  367.6 2.5 convert_reduce_fusion.1
  370.2 2.3 fusion.35
  374.1 4.9 convolution_bitcast_fusion
  379.0 8.1 copy.96
  388.5 7.2 fusion.41
  396.8 8.2 fusion.55
  405.0 1.4 copy-done.22
  406.4 5.4 add_bitcast_fusion
  411.8 110.0 %all-reduce.21.cloned.1.call-done = (f32[12,1024]{1,0:T(8,128)}, f32[2304]{0:T(1024)}, f32[768]{0:T(1024)}, f32[768]{0:T(1024)}, f32[768]{0:T(1024)}, /*index=5*...) async-done(((f32[12,1024]{1,0:T(8,128)}, f32[2304]{0:T(1024)}, f32[768]{0:T(1024)}, f32[768]{0:T(1024)}, f32[768]{0:T(1024)}, /*index=5*/f32[3072]{0:T(1024)}, ...) | async-done | bytes 89104 | tf_op jit(solution)/shard_map/psum | solution.py:396
  521.8 1.3 dynamic-slice.1
  524.4 1.3 dynamic-slice.3
  525.6 1.3 dynamic-slice.5
  526.9 1.3 dynamic-slice.6
  528.2 1.3 dynamic-slice.7
  529.4 1.3 dynamic-slice
  530.7 1.3 dynamic-slice.4
  532.0 96.0 %reduce-scatter.7.cloned.1.call-done = f32[24,768]{1,0:T(8,128)} async-done(((f32[768,768]{1,0:T(8,128)}), f32[24,768]{1,0:T(8,128)}) %reduce-scatter.7.cloned.1.call-update) | async-done | bytes 73744 | tf_op jit(solution)/shard_map/reduce_scatter | solution.py:400
  628.0 124.4 %reduce-scatter.13.cloned.1.call-done = f32[24,2304]{1,0:T(8,128)} async-done(((f32[768,2304]{1,0:T(8,128)}), f32[24,2304]{1,0:T(8,128)}) %reduce-scatter.13.cloned.1.call-update) | async-done | bytes 221200
  752.4 142.2 %reduce-scatter.9.cloned.1.call-done = f32[24,3072]{1,0:T(8,128)} async-done(((f32[768,3072]{1,0:T(8,128)}), f32[24,3072]{1,0:T(8,128)}) %reduce-scatter.9.cloned.1.call-update) | async-done | bytes 294928 | tf_op jit(solution)/shard_map/reduce_scatter | solution.py:404
  894.6 141.1 %reduce-scatter.11.cloned.1.call-done = f32[96,768]{1,0:T(8,128)} async-done(((f32[3072,768]{1,0:T(8,128)}), f32[96,768]{1,0:T(8,128)}) %reduce-scatter.11.cloned.1.call-update) | async-done | bytes 294928 | tf_op jit(solution)/shard_map/reduce_scatter | solution.py:406
  1035.7 1.5 copy.115
  (179 shorter events, 31.6 us)
Async XLA Ops:
  7.2 76.2 %copy-start = (f32[12,64,64]{2,1,0:T(8,128)S(1)}, f32[12,64,64]{2,1,0:T(8,128)}, u32[]{:S(2)}) copy-start(f32[12,64,64]{2,1,0:T(8,128)} %param.22) | copy-start | bytes 589828
  7.2 66.8 %all-gather.5.cloned.1.call-start = ((), (), s32[]{:S(2)}) async-start(), calls=%async_computation.4 | async-start | bytes 3649536 | tf_op jit(solution)/shard_map/all_gather | solution.py:254
  7.9 128.5 %all-gather.7.cloned.1.call-start = ((), (), s32[]{:S(2)}) async-start(), calls=%async_computation.5 | async-start | bytes 1216512 | tf_op jit(solution)/shard_map/all_gather | solution.py:256
  8.7 193.3 %all-gather.9.cloned.1.call-start = ((), (), s32[]{:S(2)}) async-start(), calls=%async_computation.6 | async-start | bytes 4866048 | tf_op jit(solution)/shard_map/all_gather | solution.py:260
  9.4 257.8 %all-gather.11.cloned.1.call-start = ((), (), s32[]{:S(2)}) async-start(), calls=%async_computation.7 | async-start | bytes 4866048 | tf_op jit(solution)/shard_map/all_gather | solution.py:262
  10.0 511.8 %all-reduce.21.cloned.1.call-start = ((), (), s32[]{:S(2)}) async-start(), calls=%async_computation.12 | async-start | bytes 229376 | tf_op jit(solution)/shard_map/psum | solution.py:396
  87.8 1.5 copy-start.12
  88.0 6.8 copy-start.32
  88.0 7.0 copy-start.31
  89.3 12.8 %collective-permute-start.1 = (bf16[512,1536]{1,0:T(8,128)(2,1)}, bf16[512,1536]{1,0:T(8,128)(2,1)}, u32[]{:S(2)}, u32[]{:S(2)}) collective-permute-start(bf16[512,1536]{1,0:T(8,128)(2,1)} %pad_maximum_fusion.2), channel_id=1, source_target_pairs={{2,0},{4,2},{6,4},{8,6},{10,8},{12,10},{14,12},{16,14},{18,16},{20... | collective-permute-start | bytes 4718600 | tf_op jit(solution)/shard_map/ppermute | solution.py:190
  90.6 11.6 %collective-permute-start = (bf16[512,1536]{1,0:T(8,128)(2,1)}, bf16[512,1536]{1,0:T(8,128)(2,1)}, u32[]{:S(2)}, u32[]{:S(2)}) collective-permute-start(bf16[512,1536]{1,0:T(8,128)(2,1)} %pad_maximum_fusion.2), channel_id=1, source_target_pairs={{0,2},{2,4},{4,6},{6,8},{8,10},{10,12},{12,14},{14,16},{16,18},{18... | collective-permute-start | bytes 4718600 | tf_op jit(solution)/shard_map/ppermute | solution.py:188
  95.0 13.0 %copy-start.7 = (s32[1,1536]{1,0:T(1,128)}, s32[1,1536]{1,0:T(1,128)S(1)}, u32[]{:S(2)}) copy-start(s32[1,1536]{1,0:T(1,128)S(1)} %broadcast_in_dim.25.pk_ref) | copy-start | bytes 18436
  95.1 172.1 %copy-start.35 = (f32[768]{0:T(1024)}, f32[768]{0:T(1024)S(1)}, u32[]{:S(2)}) copy-start(f32[768]{0:T(1024)S(1)} %convert_element_type.117) | copy-start | bytes 9220
  95.2 12.8 %copy-start.5 = (f32[48,1024]{1,0:T(8,128)}, f32[48,1024]{1,0:T(8,128)S(1)}, u32[]{:S(2)}) copy-start(f32[48,1024]{1,0:T(8,128)S(1)} %pad_bitcast_fusion.bias_ref) | copy-start | bytes 589828
  95.3 12.8 %copy-start.8 = (s32[1,1536]{1,0:T(1,128)}, s32[1,1536]{1,0:T(1,128)S(1)}, u32[]{:S(2)}) copy-start(s32[1,1536]{1,0:T(1,128)S(1)} %compare_select_fusion.dk_ref) | copy-start | bytes 18436
  95.3 12.7 %copy-start.4 = (s32[512,1]{1,0:T(8,128)}, s32[512,1]{1,0:T(8,128)S(1)}, u32[]{:S(2)}) copy-start(s32[512,1]{1,0:T(8,128)S(1)} %fusion.38.dq_ref) | copy-start | bytes 6148
  100.6 1.5 copy-start.13
  102.1 6.0 copy-start.1
  120.2 1.2 copy-start.6
  121.4 17.3 %copy-start.2 = (f32[512,768]{1,0:T(8,128)}, f32[512,768]{1,0:T(8,128)S(1)}, u32[]{:S(2)}) copy-start(f32[512,768]{1,0:T(8,128)S(1)} %get-tuple-element.21.att_ref) | copy-start | bytes 4718596
  138.8 1.1 copy-start.16
  140.2 127.0 %copy-start.17 = (f32[512,768]{1,0:T(8,128)S(1)}, f32[512,768]{1,0:T(8,128)}, u32[]{:S(2)}) copy-start(f32[512,768]{1,0:T(8,128)} %copy-done.16) | copy-start | bytes 4718596
  273.2 1.1 copy-start.11
  275.6 2.6 copy-start.37
  277.2 11.1 %slice-start.2 = ((s8[4718592]{0:T(1024)(128)(4,1)}), s8[4194304]{0:T(1024)(128)(4,1)S(1)}, s32[]{:S(2)}) async-start(s8[4718592]{0:T(1024)(128)(4,1)} %bitcast.121), calls=%async_computation.15 | async-start | bytes 8388608
  278.0 10.3 copy-start.29
  278.3 10.1 slice-start.3
  294.6 4.1 copy-start.21
  294.6 2.1 copy-start.38
  294.6 4.0 copy-start.33
  295.4 3.2 copy-start.23
  326.4 3.6 slice-start
  326.4 3.7 slice-start.1
  331.7 12.6 %collective-permute-start.3 = (bf16[512,1536]{1,0:T(8,128)(2,1)}, bf16[512,1536]{1,0:T(8,128)(2,1)}, u32[]{:S(2)}, u32[]{:S(2)}) collective-permute-start(bf16[512,1536]{1,0:T(8,128)(2,1)} %pad_maximum_fusion.4), channel_id=1, source_target_pairs={{2,0},{4,2},{6,4},{8,6},{10,8},{12,10},{14,12},{16,14},{18,16},{20... | collective-permute-start | bytes 4718600 | tf_op jit(solution)/shard_map/ppermute | solution.py:200
  333.0 6.4 copy-start.15
  334.3 10.0 collective-permute-start.2
  339.4 1.6 copy-start.14
  344.4 2.5 copy-start.28
  350.9 2.0 copy-start.9
  352.9 1.4 copy-start.20
  359.2 2.0 copy-start.10
  361.2 1.4 copy-start.19
  365.2 2.4 copy-start.25
  367.6 2.6 copy-start.3
  367.6 2.6 copy-start.24
  370.2 257.8 %reduce-scatter.7.cloned.1.call-start = ((), (), s32[]{:S(2)}) async-start(), calls=%async_computation.8 | async-start | bytes 2433024 | tf_op jit(solution)/shard_map/reduce_scatter | solution.py:400
  372.5 1.1 copy-start.26
  372.5 1.4 copy-start.27
  372.5 1.6 copy-start.39
  372.5 379.9 %reduce-scatter.13.cloned.1.call-start = ((), (), s32[]{:S(2)}) async-start(), calls=%async_computation.11 | async-start | bytes 7299072
  387.1 1.4 copy-start.18
  387.1 1.4 copy-start.36
  387.1 507.5 %reduce-scatter.9.cloned.1.call-start = ((), (), s32[]{:S(2)}) async-start(), calls=%async_computation.9 | async-start | bytes 9732096 | tf_op jit(solution)/shard_map/reduce_scatter | solution.py:404
  395.7 1.1 copy-start.30
  395.7 640.0 %reduce-scatter.11.cloned.1.call-start = ((), (), s32[]{:S(2)}) async-start(), calls=%async_computation.10 | async-start | bytes 9732096 | tf_op jit(solution)/shard_map/reduce_scatter | solution.py:406
  405.0 1.4 copy-start.22
  405.0 1.4 copy-start.34
Sparse Core Ops, SparseCore 0:
  10.9 62.9 all-gather.4
  76.9 59.4 all-gather.6
  139.3 62.5 all-gather.8
  204.7 62.4 all-gather.10
  370.3 151.5 all-reduce.20
  528.4 99.5 reduce-scatter.6
  634.2 118.1 reduce-scatter.12
  759.9 134.6 reduce-scatter.8
  901.0 134.5 reduce-scatter.10

commit v2 on v1

--- a/solution.py
+++ b/solution.py
@@ -173,6 +173,1134 @@
     )(dq, dk, pk, bias8, q, k, v, att, inv, ga)
 
 
+MESH = pl.DeviceIdType.MESH
+SLAB = 32
+
+
+class Place:
+    def __init__(self, n_seq):
+        self.Z = n_seq // 4
+        s, self.x = lax.axis_index("seq"), lax.axis_index("row")
+        self.s = s
+        self.c, self.y, self.z = lax.rem(s, 2), lax.rem(s // 2, 2), s // 4
+        self.me = s * 2 + self.x
+
+    def seq(self, z, y, c):
+        return (z * 2 + y) * 2 + c
+
+    def zx(self, k):
+        z, d = self.z, 1
+        while d <= k:
+            if k // d % 2:
+                z = z + d - 2 * d * lax.rem(self.z // d, 2)
+            d *= 2
+        return z
+
+    def sibling(self):
+        return (self.seq(self.z, self.y, 1 - self.c), self.x)
+
+    def xpeer(self):
+        return (self.s, 1 - self.x)
+
+    def ypeer(self):
+        return (self.seq(self.z, 1 - self.y, self.c), self.x)
+
+    def zpeer(self, k):
+        return (self.seq(self.zx(k), self.y, self.c), self.x)
+
+    def partner(self):
+        t, n = self.s - 1 + 2 * self.c, 4 * self.Z
+        return (lax.rem(t + n, n), self.x), jnp.logical_and(t >= 0, t < n)
+
+    def greet(self, partner):
+        b = pltpu.get_barrier_semaphore()
+        peers = [self.sibling(), self.xpeer(), self.ypeer()] + [self.zpeer(k) for k in range(1, self.Z)]
+        if partner:
+            peers.append(self.partner()[0])
+        for p in peers:
+            pl.semaphore_signal(b, inc=1, device_id=p, device_id_type=MESH)
+        pl.semaphore_wait(b, len(peers))
+
+
+def remote(src, dst, snd, rcv, dev):
+    return pltpu.make_async_remote_copy(src_ref=src, dst_ref=dst, send_sem=snd, recv_sem=rcv, device_id=dev, device_id_type=MESH)
+
+
+class Gather:
+    def __init__(self, place, own, G, snd, rcv, chunks):
+        self.p, self.own, self.G, self.snd, self.rcv, self.chunks = place, own, G, snd, rcv, chunks
+        self.sent = []
+
+    @staticmethod
+    def sems(Z):
+        return 5 * Z + 3
+
+    def _copy(self, k, sem, at, dev, part=None, own=False):
+        lo, n = part or self.chunks[k][:2]
+        dst = self.G.at[at + (pl.ds(lo, n),)]
+        src = self.own.at[pl.ds(lo, n)] if own else dst
+        return remote(src, dst, self.snd.at[k, sem], self.rcv.at[k, sem], dev)
+
+    def _send(self, *a, **kw):
+        c = self._copy(*a, **kw)
+        c.start()
+        self.sent.append(c)
+
+    def parts(self, k):
+        r0, rows, h = self.chunks[k]
+        return (r0, h), (r0 + h, rows - h)
+
+    def at(self, j, fy=0, fx=0):
+        p = self.p
+        return (p.zx(j), p.y if not fy else 1 - p.y, p.c, p.x if not fx else 1 - p.x)
+
+    def column(self, k, t, other=False):
+        p = self.p
+        y, x = (1 - p.y if t > 1 else p.y), (1 - p.x if t % 2 else p.x)
+        return self._copy(k, 5 * p.Z - 1 + t, (slice(None), y, 1 - p.c if other else p.c, x), p.sibling())
+
+    def give(self, k, t):
+        c = self.column(k, t)
+        c.start()
+        self.sent.append(c)
+
+    def bz(self, k):
+        for j in range(1, self.p.Z):
+            self._send(k, j - 1, self.at(0), self.p.zpeer(j), own=True)
+
+    def bx(self, k):
+        self._send(k, self.p.Z - 1, self.at(0), self.p.xpeer(), own=True)
+
+    def by(self, k):
+        self._send(k, 2 * self.p.Z - 1, self.at(0), self.p.ypeer(), own=True)
+
+    def direct(self, k, j):
+        p, (lo, n) = self.p, self.chunks[k][:2]
+        for sem, dev in ((p.Z - 1 + j, p.xpeer()), (2 * p.Z - 1 + j, p.ypeer())):
+            at = self.at(j) + (pl.ds(lo, n),)
+            c = remote(self.own.at[p.zx(j), pl.ds(lo, n)], self.G.at[at], self.snd.at[k, sem], self.rcv.at[k, sem], dev)
+            c.start()
+            self.sent.append(c)
+
+    def pzx(self, k):
+        p, Z = self.p, self.p.Z
+        for j in range(1, Z):
+            self._copy(k, j - 1, self.at(j), p.zpeer(j)).wait_recv()
+            self._send(k, Z - 1 + j, self.at(j), p.xpeer())
+        self.give(k, 0)
+
+    def pzy(self, k):
+        for j in range(1, self.p.Z):
+            self._send(k, 2 * self.p.Z - 1 + j, self.at(j), self.p.ypeer())
+
+    def px(self, k):
+        p, Z = self.p, self.p.Z
+        a, b = self.parts(k)
+        for j in range(Z):
+            self._copy(k, Z - 1 + j, self.at(j, 0, 1), p.xpeer()).wait_recv()
+            if a[1]:
+                self._send(k, 3 * Z - 1 + j, self.at(j, 0, 1), p.ypeer(), a)
+            self._copy(k, 2 * Z - 1 + j, self.at(j, 1, 0), p.ypeer()).wait_recv()
+            if b[1]:
+                self._send(k, 4 * Z - 1 + j, self.at(j, 1, 0), p.xpeer(), b)
+        self.give(k, 1)
+        self.give(k, 2)
+
+    def pd(self, k):
+        p, Z = self.p, self.p.Z
+        a, b = self.parts(k)
+        for j in range(Z):
+            if a[1]:
+                self._copy(k, 3 * Z - 1 + j, self.at(j, 1, 1), p.ypeer(), a).wait_recv()
+            if b[1]:
+                self._copy(k, 4 * Z - 1 + j, self.at(j, 1, 1), p.xpeer(), b).wait_recv()
+        self.give(k, 3)
+
+    def fin(self, k):
+        for t in range(4):
+            self.column(k, t, True).wait_recv()
+
+    def drain(self):
+        for c in self.sent:
+            c.wait_send()
+        self.sent = []
+
+
+def play(steps, table):
+    for step in steps:
+        name = step.rstrip("0123456789")
+        table[name](int(step[len(name):]))
+
+
+class Scatter:
+    def __init__(self, place, sib, own, R0, R1, R2, R3, snd, rcv, chunks):
+        self.p, self.sib, self.own, self.R0, self.R1, self.R2, self.R3 = place, sib, own, R0, R1, R2, R3
+        self.snd, self.rcv, self.chunks = snd, rcv, chunks
+        self.sent = []
+
+    @staticmethod
+    def sems(Z):
+        return 6 * Z - 1
+
+    @staticmethod
+    def buffers(Z, R, W):
+        return [pltpu.VMEM((2 * Z, 2, R, W), BF16), pltpu.VMEM((Z, 2, R, W), BF16), pltpu.VMEM((Z, R, W), BF16), pltpu.VMEM((Z - 1, R, W), BF16)]
+
+    def rows(self, k):
+        return pl.ds(*self.chunks[k][:2])
+
+    def parts(self, k):
+        r0, n, h = self.chunks[k]
+        return pl.ds(r0, h) if h else None, pl.ds(r0 + h, n - h) if h < n else None
+
+    def _go(self, src, dst, k, sem, dev, start):
+        c = remote(src, dst, self.snd.at[k, sem], self.rcv.at[k, sem], dev)
+        if start:
+            c.start()
+            self.sent.append(c)
+        else:
+            c.wait_recv()
+
+    def order(self):
+        return list(range(self.p.Z - 1, -1, -1))
+
+    def _c0(self, k, j, start):
+        zy = pl.ds(2 * self.p.zx(j), 2)
+        self._go(self.sib(k, zy), self.R0.at[zy, :, self.rows(k)], k, j, self.p.sibling(), start)
+
+    def _c1(self, k, j, start):
+        p = self.p
+        z = p.zx(j)
+        a, b = self.parts(k)
+        if a is not None:
+            self._go(self.R0.at[pl.ds(2 * z, 2), 1 - p.x, a], self.R1.at[z, :, a], k, p.Z + j, p.xpeer(), start)
+        if b is not None:
+            self._go(self.R0.at[2 * z + 1 - p.y, :, b], self.R1.at[z, :, b], k, 2 * p.Z + j, p.ypeer(), start)
+
+    def _c2(self, k, j, start):
+        p = self.p
+        z = p.zx(j)
+        a, b = self.parts(k)
+        if a is not None:
+            self._go(self.R1.at[z, 1 - p.y, a], self.R2.at[z, a], k, 3 * p.Z + j, p.ypeer(), start)
+        if b is not None:
+            self._go(self.R1.at[z, 1 - p.x, b], self.R2.at[z, b], k, 4 * p.Z + j, p.xpeer(), start)
+
+    def _c3(self, k, j, start):
+        r = self.rows(k)
+        self._go(self.R2.at[self.p.zx(j), r], self.R3.at[j - 1, r], k, 5 * self.p.Z + j - 1, self.p.zpeer(j), start)
+
+    def begin(self, k):
+        for j in self.order():
+            self._c0(k, j, True)
+
+    @staticmethod
+    def _add(dst, src):
+        dst[...] = (dst[...].astype(F32) + src[...].astype(F32)).astype(BF16)
+
+    def core(self, k, js=None):
+        p = self.p
+        for j in js or self.order():
+            self._c0(k, j, False)
+            z = p.zx(j)
+            for y in range(2):
+                for x in range(2):
+                    self._add(self.R0.at[2 * z + y, x, self.rows(k)], self.own(k, 2 * z + y, x))
+            self._c1(k, j, True)
+
+    def one(self, k, js=None):
+        p = self.p
+        a, b = self.parts(k)
+        for j in js or self.order():
+            self._c1(k, j, False)
+            z = p.zx(j)
+            for i in range(2):
+                if a is not None:
+                    self._add(self.R1.at[z, i, a], self.R0.at[2 * z + i, p.x, a])
+                if b is not None:
+                    self._add(self.R1.at[z, i, b], self.R0.at[2 * z + p.y, i, b])
+            self._c2(k, j, True)
+
+    def two(self, k, js=None):
+        p = self.p
+        a, b = self.parts(k)
+        for j in js or self.order():
+            self._c2(k, j, False)
+            z = p.zx(j)
+            if a is not None:
+                self._add(self.R2.at[z, a], self.R1.at[z, p.y, a])
+            if b is not None:
+                self._add(self.R2.at[z, b], self.R1.at[z, p.x, b])
+            if j:
+                self._c3(k, j, True)
+
+    def finish(self, k):
+        p, r = self.p, self.rows(k)
+        total = self.R2[p.z, r].astype(F32)
+        for j in range(1, p.Z):
+            self._c3(k, j, False)
+            total = total + self.R3[j - 1, r].astype(F32)
+        return total
+
+    def drain(self):
+        for c in self.sent:
+            c.wait_send()
+        self.sent = []
+
+
+class SumAll:
+    def __init__(self, place, cur, got, snd, rcv):
+        self.p, self.cur, self.got, self.snd, self.rcv = place, cur, got, snd, rcv
+        p = place
+        self.peers = [p.sibling(), p.xpeer(), p.ypeer()]
+        d = 1
+        while d < p.Z:
+            self.peers.append(p.zpeer(d))
+            d *= 2
+
+    @staticmethod
+    def steps(Z):
+        return 3 + (Z - 1).bit_length()
+
+    def _copy(self, i):
+        return remote(self.cur.at[i], self.got.at[i], self.snd.at[i], self.rcv.at[i], self.peers[i])
+
+    def start(self, i):
+        self._copy(i).start()
+
+    def step(self, i):
+        self._copy(i).wait()
+        self.cur[i + 1] = self.cur[i] + self.got[i]
+
+
+def dma(*shape):
+    return pltpu.SemaphoreType.DMA(shape)
+
+
+def vmem(*n):
+    return [pl.BlockSpec(memory_space=pltpu.VMEM)] * (n[0] if n else 1)
+
+
+def doc_numbers(len_ref, pos):
+    ends, count = jnp.int32(0), jnp.zeros(pos.shape, jnp.int32)
+    for i in range(len_ref.shape[1]):
+        ends = ends + len_ref[0, i]
+        count = count + jnp.where(pos >= ends, 1, 0)
+    return jnp.where(pos < 0, -1, count)
+
+
+def fill_band(mask_s, len_ref, pk, start, half):
+    S, span = mask_s.shape
+    KS = pk.shape[1]
+    dk = doc_numbers(len_ref, start - half + lax.broadcasted_iota(jnp.int32, (1, KS), 1))
+    for a in range(S // SB):
+        dq = doc_numbers(len_ref, start + a * SB + lax.broadcasted_iota(jnp.int32, (SB, 1), 0))
+        r = lax.broadcasted_iota(jnp.int32, (SB, span), 0)
+        c = lax.broadcasted_iota(jnp.int32, (SB, span), 1)
+        ok = (dq == dk[:, a * SB:a * SB + span]) & ((pk[:, a * SB:a * SB + span] == 1) | (c == r + half))
+        mask_s[a * SB:(a + 1) * SB, :] = jnp.where(ok, 1.0, 0.0)
+
+
+def fill_features(dm_s, draws_ref):
+    m, d = draws_ref.shape[1:]
+    z = jnp.zeros((m, d), F32)
+    for i in range(draws_ref.shape[0] // 2):
+        full = jnp.concatenate([jnp.concatenate([draws_ref[2 * i], z], 1), jnp.concatenate([z, draws_ref[2 * i + 1]], 1)], 0)
+        dm_s[0, i], dm_s[1, i] = split2(full)
+
+
+def ones_per_head():
+    lane = lax.broadcasted_iota(jnp.int32, (256, 128), 1) // 64
+    row = lax.rem(lax.broadcasted_iota(jnp.int32, (256, 128), 0) // 64, 2)
+    return jnp.where(lane == row, 1.0, 0.0).astype(BF16)
+
+
+def split2(x):
+    hi = x.astype(BF16)
+    return hi, (x - hi.astype(F32)).astype(BF16)
+
+
+def coefs(bias_ref, i, t_s, span):
+    for h in range(2):
+        t_s[h * SB:(h + 1) * SB, :] = toep(jnp.exp(bias_ref[pl.ds(2 * i + h, 1), :]), span)
+
+
+FORWARD = (
+    "bx1", "by0", "bx2", "bx0", "bz0", "bz1", "by1", "by2", "bz2", "bz3", "pzx0", "pzy0", "px0", "bz4", "pzx1", "pzy1", "by3",
+    "pd0", "H0", "px1", "pzx2", "pzy2", "pd1", "fin0", "pre0", "bx5", "bx4", "bx3", "po0", "bz5", "px2", "fin1", "po1", "pzx4",
+    "pzx3", "pzy3", "pd2", "fin2", "pzx5", "po2", "KV0", "dz0", "hw0", "px3", "mask0", "by4", "kvw0", "pzy4", "by5", "rim0", "pr0",
+    "px4", "pzy5", "rim1", "pr1", "pd3", "px5", "pd4", "rim2", "pr2", "pd5", "fin4", "fin3", "fin5", "uo0", "uu0", "uu1", "dw0",
+)
+CUT_FORWARD = (0, 0, 0, 0, 0, 0)
+
+
+def phi(z, dh, dl, on, scale):
+    s = z * scale
+    sh, sl = split2(s)
+    rows = dot(jnp.concatenate([sh, sl], 1), jnp.concatenate([dh, dh], 1), NT) + dot(sh, dl, NT)
+    half = dot(jnp.concatenate(split2(s * s * 0.5), 1), on)
+    return jnp.exp(rows - half) * (dh.shape[0] // 2) ** -0.5
+
+
+def fwd_attend(S, span, i, bias_ref, q_s, k_s, v_s, mask_s, t_s, w_s, vv_s, att_ref, inv_ref):
+    lanes = pl.ds(pl.multiple_of(i * 128, 128), 128)
+    CH = span // 3
+    coefs(bias_ref, i, t_s, span)
+    vv_s[:, :128] = v_s[:, lanes]
+    for a in range(S // SB):
+        rs = slice(a * SB, (a + 1) * SB)
+        qq = jnp.concatenate(halves(q_s[S + a * SB:S + (a + 1) * SB, lanes]), 0)
+        for c in range(0, span, CH):
+            s = dot(qq, k_s[a * SB + c:a * SB + c + CH, lanes], NT)
+            m = mask_s[rs, c:c + CH]
+            for h in range(2):
+                hs = slice(h * SB, (h + 1) * SB)
+                w_s[hs, c:c + CH] = (s[hs] * (t_s[hs, c:c + CH] * m)).astype(BF16)
+        o = dot(w_s[...], vv_s[a * SB:a * SB + span, :])
+        inv = 1.0 / pick(o[:SB, 128:], o[SB:, 128:])
+        att_ref[rs, lanes] = pick(o[:SB, :128], o[SB:, :128]) * inv
+        inv_ref[rs, lanes] = inv
+
+
+def forward_kernel(n_seq, chunks, scale, wq_ref, wo_ref, wu_ref, wd_ref, b3_ref, b4_ref, b1_ref, x_ref, pad_ref, bias_ref, draws_ref, len_ref,
+                   qkv_h, out_h, up_h, zq_h, zk_h, q_h, k_h, v_h, att_h, inv_h, vec_ref, pk_ref, col_ref,
+                   qkv_ref, out_ref, up_ref, zq_ref, zk_ref, q_ref, k_ref, v_ref, att_ref, inv_ref,
+                   own_s, G, XR, P3, pad_s, mask_s, t_s, w_s, vv_s, dm_s, snd, rcv, hsnd, hrcv, dsnd, drcv, osem):
+    S, W = x_ref.shape
+    f = wo_ref.shape[0]
+    win = bias_ref.shape[1]
+    span = win + SB
+    wide = 256
+    p = Place(n_seq)
+    g = Gather(p, own_s, G, snd, rcv, chunks)
+
+    def placed(v, n):
+        return pltpu.roll(jnp.broadcast_to(v, (8, v.shape[1])), p.me * n, 1)[:1]
+
+    def thirds(v, j):
+        return jnp.concatenate([v[:, t * W + j * wide:t * W + (j + 1) * wide] for t in range(3)], 1)
+
+    wq = wq_ref[...].astype(F32)
+    b3 = placed(b3_ref[...], 3 * f)
+    b4 = placed(b4_ref[...], 4 * f)
+    singles = pltpu.roll(b1_ref[...], p.me * f, 1)
+    rest = [[b4[:, j * W:(j + 1) * W] for j in range(4)] + [singles[0:3]], [singles[3:6], jnp.zeros((4, W), F32)], [jnp.zeros((7, W), F32)]]
+    for j in range(3):
+        own_s[j * SLAB:(j + 1) * SLAB, :] = jnp.concatenate([thirds(wq, j), thirds(b3, j)] + rest[j], 0).astype(BF16)
+    wide_up = [wu_ref[:, j * W:(j + 1) * W].astype(F32) for j in range(4)]
+    own_s[3 * SLAB:4 * SLAB, :] = jnp.concatenate([wo_ref[...].astype(F32), jnp.zeros((SLAB - f, W), F32)], 0).astype(BF16)
+    own_s[4 * SLAB:, :] = jnp.concatenate(wide_up, 0).astype(BF16)
+    pad_s[...] = jnp.broadcast_to(pad_ref[...], pad_s.shape)
+    p.greet(True)
+    partner, has = p.partner()
+    mine, theirs = 2 * p.c, 2 - 2 * p.c
+    leaving = []
+
+    def leave(src, dst):
+        c = pltpu.make_async_copy(src, dst, osem.at[len(leaving)])
+        c.start()
+        leaving.append(c)
+
+    halo = (remote(x_ref, XR, hsnd.at[0], hrcv.at[0], partner), remote(pad_s, P3.at[theirs], hsnd.at[1], hrcv.at[1], partner))
+    halo_in = remote(pad_s, P3.at[mine], hsnd.at[1], hrcv.at[1], partner)
+    pads = remote(pad_s, P3.at[mine], hsnd.at[2], hrcv.at[2], p.sibling())
+    pads_in = remote(pad_s, P3.at[theirs], hsnd.at[2], hrcv.at[2], p.sibling())
+    own_rows, far, near = pl.ds(S, S), pl.ds(pl.multiple_of(mine * S, S), S), pl.ds(pl.multiple_of(theirs * S, S), S)
+    given = [remote(r.at[own_rows], r.at[far], hsnd.at[3 + i], hrcv.at[3 + i], p.sibling()) for i, r in enumerate((k_ref, v_ref, q_ref))]
+    taken = [remote(r.at[own_rows], r.at[near], hsnd.at[3 + i], hrcv.at[3 + i], p.sibling()) for i, r in enumerate((k_ref, v_ref, q_ref))]
+    pads.start()
+
+    def send_halo(_):
+        @pl.when(has)
+        def _():
+            for h in halo:
+                h.start()
+
+    def take_halo(_):
+        @pl.when(has)
+        def _():
+            halo[0].wait_recv()
+            halo_in.wait_recv()
+
+        @pl.when(jnp.logical_not(has))
+        def _():
+            XR[...] = jnp.zeros_like(XR)
+            P3[mine] = jnp.zeros(pad_s.shape, jnp.int32)
+
+    G[p.z, p.y, p.c, p.x] = own_s[...]
+    P3[1] = pad_s[...]
+
+    def down(j):
+        return remote(wd_ref, col_ref.at[p.z], dsnd.at[j - 1], drcv.at[j - 1], p.zpeer(j))
+
+    def down_in(j):
+        return remote(wd_ref, col_ref.at[p.zx(j)], dsnd.at[j - 1], drcv.at[j - 1], p.zpeer(j))
+
+    def send_down(_):
+        for j in range(1, p.Z):
+            down(j).start()
+
+    def take_down(_):
+        for j in range(1, p.Z):
+            down_in(j).wait_recv()
+
+    col_ref[p.z] = wd_ref[...]
+
+    def early(_):
+        fill_features(dm_s, draws_ref)
+        vv_s[:, 128:] = jnp.ones((vv_s.shape[0], 128), BF16)
+
+    on = ones_per_head()
+
+    def features(z, i):
+        return phi(z, dm_s[0, i], dm_s[1, i], on, scale).astype(BF16)
+
+    def project(j):
+        cs = slice(j * wide, (j + 1) * wide)
+        unpack_qkv(g, j, qkv_ref, vec_ref)
+        bias = vec_ref[8 * j:8 * j + 1, :]
+        x = x_ref[...]
+        zq = dot(x, qkv_ref[j, :, :wide]) + bias[:, :wide]
+        zk = dot(x, qkv_ref[j, :, wide:2 * wide]) + bias[:, wide:2 * wide]
+        zq_ref[:, cs] = zq
+        zk_ref[:, cs] = zk
+        for i in range(wide // 128):
+            pp, at = wide // 128 * j + i, slice(i * 128, (i + 1) * 128)
+            lanes = slice(pp * 128, (pp + 1) * 128)
+            q_ref[S:2 * S, lanes] = features(zq[:, at], pp)
+            k_ref[S:2 * S, lanes] = features(zk[:, at], pp)
+        v_ref[S:2 * S, cs] = (dot(x, qkv_ref[j, :, 2 * wide:]) + bias[:, 2 * wide:]).astype(BF16)
+        leave(qkv_ref.at[j], qkv_h.at[j])
+        for a, b in ((zq_ref, zq_h), (zk_ref, zk_h)):
+            leave(a.at[:, cs], b.at[:, cs])
+
+    def give(_):
+        for c in given:
+            c.start()
+
+    def band(_):
+        pads_in.wait_recv()
+        pk_ref[...] = jnp.concatenate([P3[0, :1], P3[1, :1], P3[2, :1]], 1)
+        fill_band(mask_s, len_ref, pk_ref[...], p.s * S, win // 2)
+
+    def rim(j):
+        cs = slice(j * wide, (j + 1) * wide)
+        bias = vec_ref[8 * j:8 * j + 1, :]
+        x = XR[...]
+        zq = dot(x, qkv_ref[j, :, :wide]) + bias[:, :wide]
+        zk = dot(x, qkv_ref[j, :, wide:2 * wide]) + bias[:, wide:2 * wide]
+        for i in range(wide // 128):
+            pp = wide // 128 * j + i
+            q_ref[far, pp * 128:(pp + 1) * 128] = features(zq[:, i * 128:(i + 1) * 128], pp)
+            k_ref[far, pp * 128:(pp + 1) * 128] = features(zk[:, i * 128:(i + 1) * 128], pp)
+        v_ref[far, cs] = (dot(x, qkv_ref[j, :, 2 * wide:]) + bias[:, 2 * wide:]).astype(BF16)
+        if j == 2:
+            for a, b in ((q_ref, q_h), (k_ref, k_h), (v_ref, v_h)):
+                leave(a, b)
+
+    def take(_):
+        for c in taken:
+            c.wait_recv()
+
+    def pairs(j):
+        def pair(i, _):
+            fwd_attend(S, span, i, bias_ref, q_ref, k_ref, v_ref, mask_s, t_s, w_s, vv_s, att_ref, inv_ref)
+            return 0
+
+        lax.fori_loop(2 * j, 2 * j + 2, pair, 0)
+        cs = slice(j * wide, (j + 1) * wide)
+        for a, b in ((att_ref, att_h), (inv_ref, inv_h)):
+            leave(a.at[:, cs], b.at[:, cs])
+
+    def unpack_up(i):
+        k = 4 + i
+        lo, n, _ = chunks[k]
+        first = (lo - 4 * SLAB) // f
+
+        def put(at, j, v):
+            up_ref[at, (first + j) * W:(first + j + 1) * W] = v
+
+        shard_pairs(G, lo, n, f, put)
+        cs = slice(first * W, first * W + n // f * W)
+        leave(up_ref.at[:, cs], up_h.at[:, cs])
+
+    def unpack_out(_):
+        def put(at, j, v):
+            out_ref[at, :] = v
+
+        shard_pairs(G, 3 * SLAB, f, f, put)
+        leave(out_ref, out_h)
+
+    play(FORWARD, dict(
+        bx=g.bx, by=g.by, bz=g.bz, pzx=g.pzx, pzy=g.pzy, px=g.px, pd=g.pd, fin=g.fin, H=send_halo, hw=take_halo, pre=early, po=project,
+        KV=give, kvw=take, mask=band, rim=rim, pr=pairs, uo=unpack_out, uu=unpack_up, dz=send_down, dw=take_down))
+
+    @pl.when(has)
+    def _():
+        for h in halo:
+            h.wait_send()
+    for c in given + [pads] + [down(j) for j in range(1, p.Z)]:
+        c.wait_send()
+    g.drain()
+    for c in leaving:
+        c.wait()
+
+
+def shard_pairs(G, lo, n, f, put):
+    def one(s, _):
+        full = pl.ds(lo, (n + 15) // 16 * 16)
+        at = (s // 4, lax.rem(s // 2, 2), lax.rem(s, 2))
+        a, b = (G[at + (x, full)].astype(F32) for x in range(2))
+        rows = pl.ds(pl.multiple_of(s * 2 * f, 2 * f), 2 * f)
+        for j in range(n // f):
+            put(rows, j, jnp.concatenate([a[j * f:(j + 1) * f], b[j * f:(j + 1) * f]], 0).astype(BF16))
+        return 0
+
+    lax.fori_loop(0, 4 * G.shape[0], one, 0)
+
+
+def unpack_qkv(g, j, qkv_ref, vec_ref):
+    G = g.G
+    f = qkv_ref.shape[1] // (8 * G.shape[0])
+    lo = j * SLAB
+
+    def one(s, t):
+        at = (s // 4, lax.rem(s // 2, 2), lax.rem(s, 2))
+        a, b = (G[at + (x, pl.ds(lo, SLAB))].astype(F32) for x in range(2))
+        qkv_ref[j, pl.ds(pl.multiple_of(s * 2 * f, 2 * f), 2 * f), :] = jnp.concatenate([a[:f], b[:f]], 0).astype(BF16)
+        return t + a[f:] + b[f:]
+
+    vec_ref[8 * j:8 * j + 8, :] = lax.fori_loop(0, 4 * G.shape[0], one, jnp.zeros((SLAB - f, G.shape[-1]), F32))
+
+
+def forward(n_seq, wq, wo, wu, wd, b3, b4, b1, x, pad, bias, draws, lens):
+    S, W = x.shape
+    f = wo.shape[0]
+    win = bias.shape[1]
+    span = win + SB
+    KS = S + win
+    Z = n_seq // 4
+    R = 4 * SLAB + 4 * f
+    chunks = tuple((SLAB * k, SLAB, CUT_FORWARD[k]) for k in range(4)) + tuple((4 * SLAB + 2 * f * k, 2 * f, CUT_FORWARD[4 + k]) for k in range(2))
+    V = pltpu.VMEM
+    M = Gather.sems(Z)
+    D = f * 2 * n_seq
+    sd = jax.ShapeDtypeStruct
+    heads, feats, dims = draws.shape
+    K = len(chunks)
+    large = (sd((3, D, W), BF16), sd((D, W), BF16), sd((D, 4 * W), BF16), sd((S, W), F32), sd((S, W), F32),
+             sd((KS, W), BF16), sd((KS, W), BF16), sd((KS, W), BF16), sd((S, W), F32), sd((S, W), F32))
+    return pl.pallas_call(
+        functools.partial(forward_kernel, n_seq, chunks, dims ** -0.25),
+        out_shape=large + (sd((24, W), F32), sd((1, KS), jnp.int32), sd((Z, 4 * f, W), BF16)),
+        in_specs=vmem(11) + [pl.BlockSpec(memory_space=pltpu.SMEM)], out_specs=(pl.BlockSpec(memory_space=pl.ANY),) * len(large) + tuple(vmem(3)),
+        scratch_shapes=[V(s.shape, s.dtype) for s in large] + [
+            V((R, W), BF16), V((Z, 2, 2, 2, R, W), BF16), V((S, W), BF16), V((3, 8, S), jnp.int32), V((8, S), jnp.int32),
+            V((S, span), F32), V((2 * SB, span), F32), V((2 * SB, span), BF16), V((KS, 256), BF16),
+            V((2, heads // 2, 2 * feats, 2 * dims), BF16), dma(K, M), dma(K, M), dma(6), dma(6), dma(Z - 1), dma(Z - 1), dma(24)],
+        compiler_params=pltpu.CompilerParams(collective_id=1, has_side_effects=True, vmem_limit_bytes=60 << 20),
+        name="forward",
+    )(wq, wo, wu, wd, b3, b4, b1, x, pad, bias, draws, lens)
+
+
+DOWN_PARTS = 3
+CUT_DOWN = 16
+
+
+def lane_mean(v):
+    return jnp.mean(v, 1, keepdims=True)
+
+
+def rows_loop(total, step, body):
+    def one(i, c):
+        body(pl.ds(pl.multiple_of(i * step, step), step))
+        return c
+
+    lax.fori_loop(0, total // step, one, 0)
+
+
+def fold8(v):
+    return jnp.sum(v.reshape(v.shape[0] // 8, 8, v.shape[1]), 0)
+
+
+def normal_cdf_pdf(x):
+    u = jnp.abs(x) * 0.7071067811865476
+    t = 1.0 / (1.0 + 0.3275911 * u)
+    e = jnp.exp(-0.5 * x * x)
+    poly = t * (0.254829592 + t * (-0.284496736 + t * (1.421413741 + t * (-1.453152027 + t * 1.061405429))))
+    tail = 0.5 * poly * e
+    return jnp.where(x >= 0, 1.0 - tail, tail), e * 0.3989422804014327
+
+
+def middle_kernel(n_seq, heads, col_ref, x_ref, vec_ref, ct_h, att_h, inv_h, ow_h, up_h, out_ref, g1_ref, gw_ref, gt_ref, vg_ref, P_h,
+                  ct_ref, att_ref, inv_ref, ow_ref, up_ref, P_ref,
+                  al_s, hl_s, hlt_s, h1_s, n1_s, i1_s, act_s, dg_s, gi_s, r_s, gl_s, acc_s, G, snd, rcv, lsem, osem):
+    S, W = x_ref.shape
+    FF_ = up_ref.shape[1]
+    n_dev = P_ref.shape[0]
+    f = W // n_dev
+    RB = 64
+    p = Place(n_seq)
+    loads = [pltpu.make_async_copy(a, b, lsem.at[i]) for i, (a, b) in enumerate(
+        ((att_h, att_ref), (ow_h, ow_ref), (up_h, up_ref), (ct_h, ct_ref), (inv_h, inv_ref)))]
+    for c in loads:
+        c.start()
+    part = 4 * f // DOWN_PARTS
+    g = Gather(p, col_ref, G, snd, rcv, tuple((part * k, part, CUT_DOWN) for k in range(DOWN_PARTS)))
+    p.greet(False)
+    G[:, p.y, p.c, p.x] = col_ref[...]
+    for k in range(DOWN_PARTS):
+        for j in range(p.Z):
+            g.direct(k, j)
+    for k in range(DOWN_PARTS):
+        g.give(k, 0)
+    b_out, gain_a, shift_a, b_down, gain_f, shift_f = (vec_ref[i:i + 1] for i in (5, 6, 7, 9, 10, 11))
+    acc_s[...] = jnp.zeros_like(acc_s)
+
+    def cast(rs):
+        al_s[rs, :] = att_ref[rs, :].astype(BF16)
+
+    loads[0].wait()
+    rows_loop(S, RB, cast)
+    loads[1].wait()
+    r_s[...] = dot(al_s[...], ow_ref[...])
+
+    def norm_one(rs):
+        r = r_s[rs, :] + (x_ref[rs, :].astype(F32) + b_out)
+        c = r - lane_mean(r)
+        inv = lax.rsqrt(lane_mean(c * c) + EPS)
+        n = c * inv
+        n1_s[rs, :] = n
+        i1_s[rs, :] = jnp.broadcast_to(inv, (RB, 128))
+        h = n * gain_a + shift_a
+        h1_s[rs, :] = h
+        hl_s[rs, :] = h.astype(BF16)
+
+    rows_loop(S, RB, norm_one)
+    loads[2].wait()
+    hlt_s[...] = hl_s[...].T
+    CW = W // 2
+    between = {1: ((g.px, 0),), 2: ((g.px, 1),), 3: ((g.px, 2),), 5: ((g.pd, 0),), 6: ((g.pd, 1),), 7: ((g.pd, 2),)}
+    for j in range(FF_ // CW):
+        cs = slice(j * CW, (j + 1) * CW)
+        inner = dot(hl_s[...], up_ref[:, cs]) + vec_ref[1 + j // 2:2 + j // 2, j % 2 * CW:(j % 2 + 1) * CW]
+        cdf, pdf = normal_cdf_pdf(inner)
+        act_s[:, cs] = (inner * cdf).astype(BF16)
+        dg_s[:, cs] = cdf + inner * pdf
+        for step, k in between.get(j, ()):
+            step(k)
+    for k in range(DOWN_PARTS):
+        g.fin(k)
+    r_s[...] = dot(act_s[...], G[...].reshape(FF_, W))
+
+    def norm_two(rs):
+        r = r_s[rs, :] + (h1_s[rs, :] + b_down)
+        c = r - lane_mean(r)
+        inv = lax.rsqrt(lane_mean(c * c) + EPS)
+        n = c * inv
+        out_ref[rs, :] = (n * gain_f + shift_f).astype(BF16)
+        ct = ct_ref[rs, :].astype(F32)
+        acc_s[0] += fold8(ct * n)
+        acc_s[1] += fold8(ct)
+        gy = ct * gain_f
+        gr = inv * (gy - lane_mean(gy) - n * lane_mean(gy * n))
+        r_s[rs, :] = gr
+        gl = gr.astype(BF16)
+        gl_s[rs, :] = gl
+        acc_s[2] += fold8(gl.astype(F32))
+
+    loads[3].wait()
+    rows_loop(S, RB, norm_two)
+    block = FF_ // p.Z
+
+    def leave(i, lo, n):
+        rows = pl.ds(lo, n)
+        c = pltpu.make_async_copy(P_ref.at[:, rows], P_h.at[:, rows], osem.at[i])
+        c.start()
+        leaving.append(c)
+
+    leaving = []
+    per = n_dev // p.Z
+    for j in range(p.Z):
+        gd = dot(act_s[:, j * block:(j + 1) * block], gl_s[...], TN)
+        P_ref[j * per:(j + 1) * per, :4 * f, :] = gd.reshape(per, 4 * f, W).astype(BF16)
+    leave(0, 0, 4 * f)
+    vg_ref[...] = jnp.zeros_like(vg_ref)
+    for j in range(p.Z):
+        cs = slice(j * block, (j + 1) * block)
+        gi = (dot(gl_s[...], G[j].reshape(block, W), NT) * dg_s[:, cs]).astype(BF16)
+        gi_s[:, cs] = gi
+    for j in range(FF_ // W):
+        vg_ref[1 + j:2 + j, :] = jnp.sum(gi_s[:, j * W:(j + 1) * W].astype(F32), 0, keepdims=True)
+    for i in range(2):
+        parts = [dot(hlt_s[...], gi_s[:, k * W:(k + 1) * W]).reshape(n_dev, f, W) for k in (2 * i, 2 * i + 1)]
+        P_ref[:, 4 * f + 2 * f * i:4 * f + 2 * f * (i + 1), :] = jnp.concatenate(parts, 1).astype(BF16)
+        leave(1 + i, 4 * f + 2 * f * i, 2 * f)
+    r_s[...] += dot(gi_s[...], up_ref[...], NT)
+
+    def back_one(rs):
+        gr = r_s[rs, :]
+        n = n1_s[rs, :]
+        acc_s[3] += fold8(gr * n)
+        acc_s[4] += fold8(gr)
+        gy = gr * gain_a
+        inv = i1_s[rs, :1]
+        go = inv * (gy - lane_mean(gy) - n * lane_mean(gy * n))
+        g1_ref[rs, :] = go
+        gl = go.astype(BF16)
+        gl_s[rs, :] = gl
+        acc_s[5] += fold8(gl.astype(F32))
+
+    rows_loop(S, RB, back_one)
+    for row, i in ((10, 0), (11, 1), (9, 2), (6, 3), (7, 4), (5, 5)):
+        vg_ref[row:row + 1, :] = jnp.sum(acc_s[i], 0, keepdims=True)
+    go = dot(al_s[...], gl_s[...], TN).reshape(n_dev, f, W)
+    P_ref[:, 8 * f:, :] = jnp.concatenate([go, jnp.zeros((n_dev, SLAB - f, W), F32)], 1).astype(BF16)
+    leave(3, 8 * f, SLAB)
+    r_s[...] = dot(gl_s[...], ow_ref[...], NT)
+    of_head = lax.broadcasted_iota(jnp.int32, (W, 128), 0) // (W // heads) == lax.broadcasted_iota(jnp.int32, (W, 128), 1)
+    of_head = jnp.where(of_head, 1.0, 0.0).astype(BF16)
+
+    def weighted(rs):
+        g = r_s[rs, :] * inv_ref[rs, :]
+        gw_ref[rs, :] = g.astype(BF16)
+        hi, lo = split2(g * att_ref[rs, :])
+        total = -(dot(hi, of_head) + dot(lo, of_head))
+        hi = total.astype(BF16).astype(F32)
+        gt_ref[rs, :] = (hi + pltpu.roll(total - hi, heads, 1)).astype(BF16)
+
+    loads[4].wait()
+    rows_loop(S, 2 * RB, weighted)
+    g.drain()
+    for c in leaving:
+        c.wait()
+
+
+def middle(n_seq, heads, col, x, ct, att, inv, ow, up, vec):
+    S, W = x.shape
+    FF_ = up.shape[1]
+    n_dev = 2 * n_seq
+    f = W // n_dev
+    Z = n_seq // 4
+    V = pltpu.VMEM
+    sd = jax.ShapeDtypeStruct
+    return pl.pallas_call(
+        functools.partial(middle_kernel, n_seq, heads),
+        out_shape=(sd((S, W), BF16), sd((S, W), F32), sd((S, W), BF16), sd((S, 128), BF16), sd((24, W), F32), sd((n_dev, 8 * f + SLAB, W), BF16)),
+        in_specs=vmem(3) + [pl.BlockSpec(memory_space=pl.ANY)] * 5, out_specs=tuple(vmem(5)) + (pl.BlockSpec(memory_space=pl.ANY),),
+        scratch_shapes=[V((S, W), BF16), V((S, W), F32), V((S, W), F32), V((W, W), BF16), V((W, FF_), BF16), V((n_dev, 8 * f + SLAB, W), BF16),
+                        V((S, W), BF16), V((S, W), BF16), V((W, S), BF16), V((S, W), F32), V((S, W), F32), V((S, 128), F32),
+                        V((S, FF_), BF16), V((S, FF_), F32), V((S, FF_), BF16), V((S, W), F32), V((S, W), BF16), V((6, 8, W), F32),
+                        V((Z, 2, 2, 2, 4 * f, W), BF16), dma(DOWN_PARTS, Gather.sems(Z)), dma(DOWN_PARTS, Gather.sems(Z)), dma(5), dma(4)],
+        compiler_params=pltpu.CompilerParams(collective_id=2, has_side_effects=True, vmem_limit_bytes=60 << 20),
+        name="middle",
+    )(col, x, vec, ct, att, inv, ow, up)
+
+
+BACKWARD = (
+    "H0", "b3", "b0", "b1", "pre0", "c0", "b4", "pr2", "c1", "o0", "b2", "c2", "pr1", "pr0", "hw0", "o1", "v0", "c3", "ri0",
+    "t0", "o2", "t1", "pj0", "c4", "b5", "o3", "ri1", "t2", "c5", "pj1", "v1", "b6", "o4", "f1", "t3", "o5", "c6", "f0", "ri2",
+    "t4", "pj2", "b7", "v2", "t5", "o6", "c7", "t6", "v3", "f3", "o7", "t7", "f5", "v4", "f6", "f2", "f4", "gx0", "f7", "v5",
+)
+CUT_BACKWARD = (32, 32, 32, 32, 16, 16, 16, 16)
+
+
+def head_rows(gw, gt, i, heads):
+    lane = lax.broadcasted_iota(jnp.int32, gt.shape, 1)
+    rows = []
+    for h, g in enumerate(halves(gw)):
+        mine = jnp.logical_or(lane == 2 * i + h, lane == 2 * i + h + heads)
+        rows.append(jnp.concatenate([g, jnp.where(mine, gt, jnp.zeros_like(gt))], 1))
+    return jnp.concatenate(rows, 0)
+
+
+def back_own(S, span, win, heads, i, bias_ref, q_ref, k_ref, v_ref, gw_s, gt_s, mask_s, t_s, w_s, gs_s, p_s, vv_s, gkt_s, gvt_s, gq_s, bsum):
+    lanes = pl.ds(pl.multiple_of(i * 128, 128), 128)
+    CH = span // 3
+    half = win // 2
+    coefs(bias_ref, i, t_s, span)
+    vv_s[:, :128] = v_ref[:, lanes]
+    for a in range(S // SB):
+        rs, qs = slice(a * SB, (a + 1) * SB), slice(S + a * SB, S + (a + 1) * SB)
+        qq = jnp.concatenate(halves(q_ref[qs, lanes]), 0)
+        gg = head_rows(gw_s[qs, lanes], gt_s[qs, :], i, heads)
+        for c in range(0, span, CH):
+            s = dot(qq, k_ref[a * SB + c:a * SB + c + CH, lanes], NT)
+            g = dot(gg, vv_s[a * SB + c:a * SB + c + CH, :], NT)
+            m = mask_s[rs, c:c + CH]
+            for h in range(2):
+                hs = slice(h * SB, (h + 1) * SB)
+                cm = t_s[hs, c:c + CH] * m
+                w = s[hs] * cm
+                w_s[hs, c:c + CH] = w.astype(BF16)
+                gs_s[hs, c:c + CH] = (g[hs] * cm).astype(BF16)
+                pw = g[hs] * w
+                if a == 0:
+                    p_s[hs, c:c + CH] = pw
+                else:
+                    p_s[hs, c:c + CH] += pw
+        gq = dot(gs_s[...], k_ref[a * SB:a * SB + span, lanes])
+        gq_s[rs, lanes] = pick(gq[:SB], gq[SB:])
+        cols = slice(half - a * SB, half - a * SB + S)
+        gk, gv = dot(qq, gs_s[:, cols], TN), dot(gg[:, :128], w_s[:, cols], TN)
+        if a == 0:
+            gkt_s[i], gvt_s[i] = gk, gv
+        else:
+            gkt_s[i] += gk
+            gvt_s[i] += gv
+    for h in range(2):
+        bsum[pl.ds(2 * i + h, 1), :] = unskew(p_s[h * SB:(h + 1) * SB, :], win)
+
+
+def back_rim(S, span, heads, i, bias_ref, q_ref, k_ref, v_ref, gw_s, gt_s, maskr_s, t_s, w_s, gs_s, vv_s, gkt_s, gvt_s):
+    lanes = pl.ds(pl.multiple_of(i * 128, 128), 128)
+    coefs(bias_ref, i, t_s, span)
+    vv_s[S:2 * S, :128] = v_ref[S:2 * S, lanes]
+    for a in range(S // SB):
+        for side, (k0, k1, t0) in enumerate(((0, (a + 1) * SB, span - (a + 1) * SB), (a * SB, S, 0))):
+            n = k1 - k0
+            qs = slice(2 * S * side + a * SB, 2 * S * side + (a + 1) * SB)
+            qq = jnp.concatenate(halves(q_ref[qs, lanes]), 0)
+            gg = head_rows(gw_s[qs, lanes], gt_s[qs, :], i, heads)
+            s = dot(qq, k_ref[S + k0:S + k1, lanes], NT)
+            g = dot(gg, vv_s[S + k0:S + k1, :], NT)
+            m = maskr_s[side, a * SB:(a + 1) * SB, k0:k1]
+            for h in range(2):
+                hs = slice(h * SB, (h + 1) * SB)
+                cm = t_s[hs, t0:t0 + n] * m
+                w_s[hs, :n] = (s[hs] * cm).astype(BF16)
+                gs_s[hs, :n] = (g[hs] * cm).astype(BF16)
+            gkt_s[i, :, k0:k1] += dot(qq, gs_s[:, :n], TN)
+            gvt_s[i, :, k0:k1] += dot(gg[:, :128], w_s[:, :n], TN)
+
+
+def phi_back(g, feat, z, dh, dl, on, scale):
+    t = g * feat.astype(F32)
+    th, tl = split2(t)
+    back = dot(th, dh) + dot(tl, dh) + dot(th, dl)
+    total = dot(jnp.concatenate([th, tl], 1), on)
+    return scale * (back - (z * scale) * total)
+
+
+def backward_kernel(n_seq, chunks, scale, x_ref, pk_ref, bias_ref, draws_ref, len_ref, vg_ref, gw_ref, gt_ref,
+                    w_h, q_h, k_h, v_h, zq_h, zk_h, g1_h, P_h,
+                    gx_ref, rel_ref, gqkv_ref, gup_ref, gdown_ref, gout_ref, small_ref,
+                    w_ref, q_ref, k_ref, v_ref, zq_ref, zk_ref,
+                    U, PQ, R0, R1, R2, R3, mask_s, maskr_s, t_s, w_s, gs_s, p_s, vv_s, gkt_s, gvt_s, gq_s, gw_s, gt_s, gp_s, xt_s, dm_s, ex_s,
+                    cur, got, snd, rcv, hsnd, hrcv, vsnd, vrcv, lsem):
+    S, W = x_ref.shape
+    heads, win = bias_ref.shape
+    span = win + SB
+    n_pair = W // 128
+    n_dev = 2 * n_seq
+    f = W // n_dev
+    wide = 256
+    p = Place(n_seq)
+    partner, has = p.partner()
+    mine, theirs = 2 * p.c, 2 - 2 * p.c
+    far, near = pl.ds(pl.multiple_of(mine * S, S), S), pl.ds(pl.multiple_of(theirs * S, S), S)
+
+    def load(src, dst, i):
+        return pltpu.make_async_copy(src, dst, lsem.at[i])
+
+    def own_half(k):
+        r0, n = chunks[k][:2]
+        return load(P_h.at[:, p.c, :, pl.ds(r0, n)], U.at[k % 2, :, :, pl.ds(0, n)], 1 + k % 2)
+
+    residual = load(g1_h, gx_ref, 0)
+    early = [load(h, r, 3 + i) for i, (h, r) in enumerate(((q_h, q_ref), (k_h, k_ref), (v_h, v_ref)))]
+    late = [load(h, r, 6 + i) for i, (h, r) in enumerate(((zq_h, zq_ref), (zk_h, zk_ref), (w_h, w_ref)))]
+    own_half(0).start()
+    for c in early:
+        c.start()
+    own_half(1).start()
+    for c in late:
+        c.start()
+    residual.start()
+    p.greet(True)
+    sides = ((gw_ref, gw_s), (gt_ref, gt_s))
+    out_far = [remote(a, b.at[near], hsnd.at[i], hrcv.at[i], partner) for i, (a, b) in enumerate(sides)]
+    in_far = [remote(a, b.at[far], hsnd.at[i], hrcv.at[i], partner) for i, (a, b) in enumerate(sides)]
+    out_near = [remote(a, b.at[far], hsnd.at[2 + i], hrcv.at[2 + i], p.sibling()) for i, (a, b) in enumerate(sides)]
+    in_near = [remote(a, b.at[near], hsnd.at[2 + i], hrcv.at[2 + i], p.sibling()) for i, (a, b) in enumerate(sides)]
+
+    def send_halo(_):
+        for c in out_near:
+            c.start()
+
+        @pl.when(has)
+        def _():
+            for c in out_far:
+                c.start()
+
+    def take_halo(_):
+        for c in in_near:
+            c.wait_recv()
+
+        @pl.when(has)
+        def _():
+            for c in in_far:
+                c.wait_recv()
+
+    def sib(k, zy):
+        return P_h.at[zy, 1 - p.c, :, pl.ds(*chunks[k][:2])] if k < 5 else PQ.at[k - 5, zy, 1 - p.c]
+
+    def own(k, zy, x):
+        return U.at[k % 2, zy, x, pl.ds(0, chunks[k][1])] if k < 5 else PQ.at[k - 5, zy, p.c, x]
+
+    sc = Scatter(p, sib, own, R0, R1, R2, R3, snd, rcv, chunks)
+    on = ones_per_head()
+
+    def prepare(_):
+        start = p.s * S
+        fill_band(mask_s, len_ref, pk_ref[...], start, win // 2)
+        dk = doc_numbers(len_ref, start + lax.broadcasted_iota(jnp.int32, (1, S), 1))
+        real = pk_ref[:, S:2 * S] == 1
+        for side in range(2):
+            dq = doc_numbers(len_ref, start + (2 * side - 1) * S + lax.broadcasted_iota(jnp.int32, (S, 1), 0))
+            maskr_s[side] = jnp.where((dq == dk) & real, 1.0, 0.0)
+        fill_features(dm_s, draws_ref)
+        vv_s[:, 128:] = jnp.ones((vv_s.shape[0], 128), BF16)
+        gw_s[S:2 * S, :] = gw_ref[...]
+        gt_s[S:2 * S, :] = gt_ref[...]
+        xt_s[...] = x_ref[...].T
+        cur[0] = jnp.zeros(cur.shape[1:], F32)
+
+        @pl.when(jnp.logical_not(has))
+        def _():
+            gw_s[far, :] = jnp.zeros((S, W), BF16)
+            gt_s[far, :] = jnp.zeros((S, 128), BF16)
+        for c in early:
+            c.wait()
+
+    def core(k):
+        if k < 5:
+            own_half(k).wait()
+        sc.core(k)
+        if k + 2 < 5:
+            own_half(k + 2).start()
+
+    def own_pairs(j):
+        def one(i, _):
+            back_own(S, span, win, heads, i, bias_ref, q_ref, k_ref, v_ref, gw_s, gt_s, mask_s, t_s, w_s, gs_s, p_s, vv_s, gkt_s, gvt_s, gq_s, cur.at[0])
+            return 0
+
+        lax.fori_loop(2 * j, 2 * j + 2, one, 0)
+
+    def rim_pairs(j):
+        def one(i, _):
+            back_rim(S, span, heads, i, bias_ref, q_ref, k_ref, v_ref, gw_s, gt_s, maskr_s, t_s, w_s, gs_s, vv_s, gkt_s, gvt_s)
+            return 0
+
+        lax.fori_loop(2 * j, 2 * j + 2, one, 0)
+
+    def project(l):
+        if l == 0:
+            for c in late[:2]:
+                c.wait()
+
+        def one(i, _):
+            def at(t):
+                return pl.ds(pl.multiple_of(l * W + t * wide + (i - wide // 128 * l) * 128, 128), 128)
+
+            lanes = pl.ds(pl.multiple_of(i * 128, 128), 128)
+            gp_s[:, at(0)] = phi_back(gq_s[:, lanes], q_ref[S:2 * S, lanes], zq_ref[:, lanes], dm_s[0, i], dm_s[1, i], on, scale).astype(BF16)
+            gp_s[:, at(1)] = phi_back(gkt_s[i].T, k_ref[S:2 * S, lanes], zk_ref[:, lanes], dm_s[0, i], dm_s[1, i], on, scale).astype(BF16)
+            gp_s[:, at(2)] = gvt_s[i].T.astype(BF16)
+            return 0
+
+        lax.fori_loop(wide // 128 * l, wide // 128 * (l + 1), one, 0)
+        cs = slice(l * W, (l + 1) * W)
+        sums = jnp.sum(gp_s[:, cs].astype(F32), 0, keepdims=True)
+        extra = jnp.concatenate([sums, vg_ref[8 * l + 1:8 * l + 8, :]], 0)
+        part = dot(xt_s[...], gp_s[:, cs]).reshape(n_dev, f, W)
+        part = jnp.concatenate([part, jnp.broadcast_to(extra[None], (n_dev,) + extra.shape)], 1)
+        PQ[l] = part.astype(BF16).reshape(n_seq // 2, 2, 2, SLAB, W)
+
+    def tokens_back(_):
+        residual.wait()
+        late[2].wait()
+        gx_ref[...] += dot(gp_s[:, :W], w_ref[0], NT) + dot(gp_s[:, W:2 * W], w_ref[1], NT) + dot(gp_s[:, 2 * W:], w_ref[2], NT)
+
+    def done(k):
+        total = sc.finish(k)
+        if k < 2:
+            gdown_ref[2 * f * k:2 * f * (k + 1), :] = total
+        elif k < 4:
+            for j in range(2):
+                gup_ref[:, (2 * (k - 2) + j) * W:(2 * (k - 2) + j + 1) * W] = total[j * f:(j + 1) * f]
+        elif k == 4:
+            gout_ref[...] = total[:f]
+        else:
+            l = k - 5
+            for t in range(3):
+                gqkv_ref[:, t * W + l * wide:t * W + (l + 1) * wide] = total[:f, t * wide:(t + 1) * wide]
+            ex_s[8 * l:8 * l + 8, :] = total[f:]
+
+    va = SumAll(p, cur, got, vsnd, vrcv)
+    n = SumAll.steps(p.Z)
+
+    def sum_step(i):
+        if i:
+            va.step(i - 1)
+        if i < n:
+            va.start(i)
+
+    play(BACKWARD, dict(b=sc.begin, c=core, o=sc.one, t=sc.two, f=done, pre=prepare, pr=own_pairs, ri=rim_pairs, H=send_halo, hw=take_halo, pj=project, gx=tokens_back, v=sum_step))
+    rel_ref[...] = cur[n][:rel_ref.shape[0]]
+
+    def mine(row, share):
+        width = row.shape[1]
+        return pltpu.roll(jnp.broadcast_to(row, (8, width)), lax.rem(width - share * p.me, width), 1)[:1, :128]
+
+    ex = ex_s[...]
+    small_ref[0:1, :] = mine(jnp.concatenate([ex[8 * l:8 * l + 1, t * wide:(t + 1) * wide] for t in range(3) for l in range(3)], 1), 3 * f)
+    small_ref[1:2, :] = mine(jnp.concatenate([ex[k:k + 1] for k in range(1, 5)], 1), 4 * f)
+    singles = jnp.concatenate([ex[5:8], ex[9:12], jnp.zeros((2, W), F32)], 0)
+    small_ref[2:8, :] = pltpu.roll(singles, lax.rem(W - f * p.me, W), 1)[:6, :128]
+    sc.drain()
+    for c in out_near:
+        c.wait_send()
+
+    @pl.when(has)
+    def _():
+        for c in out_far:
+            c.wait_send()
+
+
+def backward(n_seq, x, pk, bias, draws, lens, w, q, k, v, vg, zq, zk, gw, gt, g1, P_):
+    S, W = x.shape
+    KS = k.shape[0]
+    heads, win = bias.shape
+    feats, dims = draws.shape[1:]
+    span = win + SB
+    Z = n_seq // 4
+    n_pair = W // 128
+    f = W // (2 * n_seq)
+    first = 8 * f + SLAB
+    R = first + 3 * SLAB
+    where = tuple((2 * f * k, 2 * f) for k in range(4)) + ((8 * f, SLAB),) + tuple((first + SLAB * l, SLAB) for l in range(3))
+    chunks = tuple(w + (h,) for w, h in zip(where, CUT_BACKWARD))
+    V = pltpu.VMEM
+    hbm = pl.BlockSpec(memory_space=pl.ANY)
+    n = SumAll.steps(Z)
+    K = len(chunks)
+    sd = jax.ShapeDtypeStruct
+    return pl.pallas_call(
+        functools.partial(backward_kernel, n_seq, chunks, dims ** -0.25),
+        out_shape=(sd((S, W), F32), sd((heads, win), F32), sd((f, 3 * W), F32), sd((f, 4 * W), F32), sd((4 * f, W), F32), sd((f, W), F32), sd((8, 128), F32)),
+        in_specs=vmem(4) + [pl.BlockSpec(memory_space=pltpu.SMEM)] + vmem(3) + [hbm] * 8, out_specs=tuple(vmem(7)),
+        scratch_shapes=[V(a.shape, a.dtype) for a in (w, q, k, v, zq, zk)] + [
+            V((2, 2 * Z, 2, 2 * f, W), BF16), V((3, 2 * Z, 2, 2, SLAB, W), BF16)] + Scatter.buffers(Z, R, W) + [
+            V((S, span), F32), V((2, S, S), F32), V((2 * SB, span), F32), V((2 * SB, span), BF16), V((2 * SB, span), BF16), V((2 * SB, span), F32),
+            V((KS, 256), BF16), V((n_pair, 128, S), F32), V((n_pair, 128, S), F32), V((S, W), F32), V((KS, W), BF16), V((KS, 128), BF16),
+            V((S, 3 * W), BF16), V((W, S), BF16),
+            V((2, heads // 2, 2 * feats, 2 * dims), BF16), V((24, W), F32), V((n + 1, 16, win), F32), V((n, 16, win), F32),
+            dma(K, Scatter.sems(Z)), dma(K, Scatter.sems(Z)), dma(4), dma(4), dma(n), dma(n), dma(9)],
+        compiler_params=pltpu.CompilerParams(collective_id=3, has_side_effects=True, vmem_limit_bytes=64 << 20),
+        name="backward",
+    )(x, pk, bias, draws, lens, vg, gw, gt, w, q, k, v, zq, zk, g1, P_)
+
 EPS = 1e-06
 EXACT_MATMUL = lax.Precision.HIGHEST
 
@@ -219,6 +1347,32 @@
     ends = jnp.cumsum(lengths_row)
     counted = jnp.sum((positions[:, None] >= ends[None, :]).astype(jnp.int32), -1)
     return jnp.where(positions < 0, -1, counted)
+
+
+def fits(n_seq, n_row, f, tokens_here, half_win):
+    return n_row == 2 and n_seq == 4 * 4 and f + 8 == SLAB and tokens_here == half_win
+
+
+def with_kernels(tokens, cotangent, lengths, padding, feature_draws, rel_bias, *weights):
+    w_qkv, b_qkv, w_out, b_out, gain_a, shift_a, w_up, b_up, w_down, b_down, gain_f, shift_f = weights
+    local = tokens[0]
+    W = local.shape[1]
+    n_seq = lax.axis_size("seq")
+    f = w_out.shape[0]
+    b3 = jnp.pad(b_qkv.astype(F32), (0, 3 * W - 3 * f))[None]
+    b4 = jnp.pad(b_up.astype(F32), (0, 4 * W - 4 * f))[None]
+    b1 = jnp.pad(jnp.stack([b_out, gain_a, shift_a, b_down, gain_f, shift_f]).astype(F32), ((0, 2), (0, W - f)))
+    (qkv_w, out_w, up_w, zq, zk, q, k, v, att, inv, vec, pk, col) = forward(
+        n_seq, w_qkv, w_out, w_up, w_down, b3, b4, b1, local, padding, rel_bias, feature_draws, lengths)
+    out, g1, gw, gt, vg, P_ = middle(n_seq, rel_bias.shape[0], col, local, cotangent[0], att, inv, out_w, up_w, vec)
+    P_ = P_.reshape(n_seq // 2, 2, 2, P_.shape[1], W)
+    gx, rel, g_qkv, g_up, g_down, g_out, small = backward(
+        n_seq, local, pk, rel_bias, feature_draws, lengths, qkv_w, q, k, v, vg, zq, zk, gw, gt, g1, P_)
+    one = [small[i, :f] for i in range(2, 8)]
+    return (
+        out[None], gx[None], rel, g_qkv, small[0, : 3 * f], g_out, one[0], one[1], one[2], g_up, small[1, : 4 * f],
+        g_down, one[3], one[4], one[5],
+    )
 
 
 def on_device(
@@ -241,6 +1395,11 @@
     gain_ffn,
     shift_ffn,
 ):
+    if fits(lax.axis_size("seq"), lax.axis_size("row"), w_out.shape[0], tokens.shape[1], rel_bias.shape[1] // 2):
+        return with_kernels(
+            tokens, cotangent, lengths, padding, feature_draws, rel_bias, w_qkv, b_qkv, w_out, b_out, gain_attn, shift_attn,
+            w_up, b_up, w_down, b_down, gain_ffn, shift_ffn,
+        )
     local = tokens[0]
     seq_len = local.shape[0]
     model_width = local.shape[1]

time: 1050 us -> 261 us (0.25)
  waiting for transfers between devices: 750 us -> 0 us
  Pallas kernels: 39.9 us -> 241 us
  matrix products: 90.4 us -> 0 us
  local copies, waits for them, and re-layouts: 62.2 us -> 11.9 us
  blocking collectives: 42.8 us -> 0 us
  other arithmetic: 31.9 us -> 2.52 us
  between operations: 15 us -> 0.9 us
  starting transfers between devices: 11.7 us -> 0 us
    reduce_scatter x3 -> x0, waiting for transfers between devices: 379 us -> none  [the longest x1 142 us: on_device(): lax.psum_scatter(grad_up_w, ('seq', 'row'), scatter_dimension=0, tiled=True)]
    pallas_call x2 -> x3, Pallas kernels: 39.9 us -> 241 us  [the longest x1 107 us: backward(): pl.pallas_call(functools.partial(backward_kernel, n_seq, chunks, dims **...]
    all_gather x4 -> x0, waiting for transfers between devices: 134 us -> none  [the longest x1 61.7 us: on_device(): lax.all_gather(w_up, ('seq', 'row'), axis=0, tiled=True)]
    unnamed x10 -> x0, waiting for transfers between devices: 127 us -> none
    psum x1 -> x0, waiting for transfers between devices: 110 us -> none  [on_device(): grad_rel = lax.psum(grad_bias, ('seq', 'row'))]
    dot_general x16 -> x0, matrix products: 90.4 us -> none  [the longest x1 20.9 us: on_device(): inner = jnp.dot(hidden_low, up_w, preferred_element_type=jnp.float32) + up_b]
    unnamed x1 -> x0, blocking collectives: 42.8 us -> none
    unnamed x114 -> x19, local copies, waits for them, and re-layouts: 39 us -> 6.61 us
  transfers between devices with their start and end apart: 13 -> 0, of which waited for: 9 -> 0; matrix products, arithmetic and copies ran while one was open for 11% -> 0% of each run, Pallas kernels for 1% -> 0%
where the time goes in v2:
time: 261 us; the launch traced here: 256 us
  Pallas kernels  241 us (92%)
  local copies, waits for them, and re-layouts  11.9 us (5%)
    pallas_call x1, Pallas kernels, backward(): pl.pallas_call(functools.partial(backward_kernel, n_seq, chunks, dims **...  107 us
    pallas_call x1, Pallas kernels, forward(): pl.pallas_call(functools.partial(forward_kernel, n_seq, chunks, dims ** (...  80.6 us
    pallas_call x1, Pallas kernels, middle(): pl.pallas_call(functools.partial(middle_kernel, n_seq, heads), out_shape=...  53.2 us
    unnamed x19, local copies, waits for them, and re-layouts  6.61 us

profile of v2, /device:TPU:0, one launch (start us, length us, event | category | flops | bytes accessed | tf_op | source)
XLA Modules:
  0.0 256.4 jit_solution(5042806529211449562)
XLA Ops:
  0.6 0.8 stack.27
  1.4 0.7 pad_convert_fusion.2
  2.1 0.6 reshape.34.b3_ref
  2.7 1.3 pad_convert_fusion.1
  3.9 0.6 pad_convert_fusion.b1_ref
  4.5 80.6 %forward.1 = (bf16[3,768,768]{2,1,0:T(8,128)(2,1)}, bf16[768,768]{1,0:T(8,128)(2,1)}, bf16[768,3072]{1,0:T(8,128)(2,1)}, f32[512,768]{1,0:T(8,128)}, f32[512,768...) custom-call(bf16[24,2304]{1,0:T(8,128)(2,1)} %wq_ref.1, ...), custom_call_target="tpu_custom_call" | custom-call | tf_op jit(solution)/shard_map/forward/pallas_call | solution.py:793
  85.1 53.2 %middle.1 = (bf16[512,768]{1,0:T(8,128)(2,1)}, f32[512,768]{1,0:T(8,128)}, bf16[512,768]{1,0:T(8,128)(2,1)}, bf16[512,128]{1,0:T(8,128)(2,1)}, f32[24,768]{1,0:T(8,128)}, /*index=5*/bf16[32,224,768]{2,1,0:T(8,128)(2,1)}) custom-call(bf16[4,96,768]{2,1,0:T(8,128)(2,1)} %get-tuple-element.41.col_ref, bf16[512,768]{1,0:T(8,128)(2,1)} %bitcast.30, ...), custom_call_target="tpu_custom_call" | custom-call | tf_op jit(solution)/shard_map/middle/pallas_call | solution.py:987
  138.3 107.3 %backward.1 = (f32[512,768]{1,0:T(8,128)}, f32[12,1024]{1,0:T(8,128)}, f32[24,2304]{1,0:T(8,128)}, f32[24,3072]{1,0:T(8,128)}, f32[96,768]{1,0:T(8,128)}, /*index=5*/f32[24,768]{1,0:T(8,128)}, f32[8,128]{1,0:T(8,128)}) custom-call(bf16[512,768]{1,0:T(8,128)(2,1)} %bitcast.31, s32[1,1536]{1,0:T(1,128)} %get-tuple-element.48.pk_ref, f32[12,1024]{1,0:T(8,128)} %bias_ref.3, ...), custom_call_target="tpu_custom_call" | custom-call | tf_op jit(solution)/shard_map/backward/pallas_call | solution.py:1289
  245.6 0.0 copy-start
  245.7 1.3 slice_bitcast_fusion.3
  247.0 1.2 slice_bitcast_fusion.7
  248.1 1.4 slice_bitcast_fusion
  249.6 2.1 copy.40
  251.6 0.0 copy-done
  251.6 0.0 copy-start.5
  251.6 0.0 copy-start.3
  251.6 0.0 copy-start.4
  251.6 0.0 copy-start.2
  251.6 0.0 copy-start.1
  251.7 1.1 copy.41
  252.8 0.0 copy-done.5
  252.8 0.6 copy.42
  253.4 0.0 copy-done.3
  253.4 0.7 copy.43
  254.1 0.0 copy-done.4
  254.1 0.6 copy.44
  254.8 0.0 copy-done.2
  254.8 0.7 copy.45
  255.5 0.0 copy-done.1
  255.5 0.7 copy.46
Async XLA Ops:
  245.6 6.0 %copy-start = (f32[512,768]{1,0:T(8,128)S(1)}, f32[512,768]{1,0:T(8,128)}, u32[]{:S(2)}) copy-start(f32[512,768]{1,0:T(8,128)} %get-tuple-element.60) | copy-start | bytes 4718596
  251.6 1.2 copy-start.5
  251.6 1.8 copy-start.3
  251.6 2.5 copy-start.4
  251.6 3.1 %copy-start.2 = (f32[24,3072]{1,0:T(8,128)S(1)}, f32[24,3072]{1,0:T(8,128)}, u32[]{:S(2)}) copy-start(f32[24,3072]{1,0:T(8,128)} %get-tuple-element.97) | copy-start | bytes 884740
  251.6 3.8 %copy-start.1 = (f32[96,768]{1,0:T(8,128)S(1)}, f32[96,768]{1,0:T(8,128)}, u32[]{:S(2)}) copy-start(f32[96,768]{1,0:T(8,128)} %get-tuple-element.99) | copy-start | bytes 884740

commit v3 on v2

--- a/solution.py
+++ b/solution.py
@@ -526,10 +526,11 @@
 
 
 FORWARD = (
-    "bx1", "by0", "bx2", "bx0", "bz0", "bz1", "by1", "by2", "bz2", "bz3", "pzx0", "pzy0", "px0", "bz4", "pzx1", "pzy1", "by3",
-    "pd0", "H0", "px1", "pzx2", "pzy2", "pd1", "fin0", "pre0", "bx5", "bx4", "bx3", "po0", "bz5", "px2", "fin1", "po1", "pzx4",
-    "pzx3", "pzy3", "pd2", "fin2", "pzx5", "po2", "KV0", "dz0", "hw0", "px3", "mask0", "by4", "kvw0", "pzy4", "by5", "rim0", "pr0",
-    "px4", "pzy5", "rim1", "pr1", "pd3", "px5", "pd4", "rim2", "pr2", "pd5", "fin4", "fin3", "fin5", "uo0", "uu0", "uu1", "dw0",
+    "bx4", "by2", "bz0", "bz1", "pre0", "bx2", "by3", "by0", "bx0", "pzx0", "by1", "bx1", "bz2", "bz3", "pzy0", "by4", "pzx1",
+    "pzy1", "pzx2", "bz5", "pzy2", "bz4", "bx5", "H0", "bx3", "px1", "px0", "px2", "pd0", "pzx5", "pd1", "fin0", "fin1", "po0",
+    "pd2", "fin2", "pzx4", "po1", "pzx3", "po2", "dz0", "KV0", "pzy3", "pzy4", "hw0", "mask0", "by5", "px3", "kvw0", "rim0",
+    "pzy5", "rim1", "px4", "rim2", "pr0", "px5", "pr1", "pd3", "pd4", "pr2", "pd5", "dw0", "fin3", "fin4", "uo0", "uu0", "fin5",
+    "uu1",
 )
 CUT_FORWARD = (0, 0, 0, 0, 0, 0)
 
@@ -544,7 +545,7 @@
 
 def fwd_attend(S, span, i, bias_ref, q_s, k_s, v_s, mask_s, t_s, w_s, vv_s, att_ref, inv_ref):
     lanes = pl.ds(pl.multiple_of(i * 128, 128), 128)
-    CH = span // 3
+    CH = span
     coefs(bias_ref, i, t_s, span)
     vv_s[:, :128] = v_s[:, lanes]
     for a in range(S // SB):
@@ -555,17 +556,17 @@
             m = mask_s[rs, c:c + CH]
             for h in range(2):
                 hs = slice(h * SB, (h + 1) * SB)
-                w_s[hs, c:c + CH] = (s[hs] * (t_s[hs, c:c + CH] * m)).astype(BF16)
-        o = dot(w_s[...], vv_s[a * SB:a * SB + span, :])
+                w_s[a % 2, hs, c:c + CH] = (s[hs] * (t_s[hs, c:c + CH] * m)).astype(BF16)
+        o = dot(w_s[a % 2], vv_s[a * SB:a * SB + span, :])
         inv = 1.0 / pick(o[:SB, 128:], o[SB:, 128:])
         att_ref[rs, lanes] = pick(o[:SB, :128], o[SB:, :128]) * inv
         inv_ref[rs, lanes] = inv
 
 
-def forward_kernel(n_seq, chunks, scale, wq_ref, wo_ref, wu_ref, wd_ref, b3_ref, b4_ref, b1_ref, x_ref, pad_ref, bias_ref, draws_ref, len_ref,
+def forward_kernel(n_seq, chunks, scale, wq_ref, wo_ref, wu_ref, wd_ref, vq_ref, vu_ref, v1_ref, v2_ref, v3_ref, v4_ref, v5_ref, v6_ref, x_ref, pad_ref, bias_ref, draws_ref, len_ref,
                    qkv_h, out_h, up_h, zq_h, zk_h, q_h, k_h, v_h, att_h, inv_h, vec_ref, pk_ref, col_ref,
                    qkv_ref, out_ref, up_ref, zq_ref, zk_ref, q_ref, k_ref, v_ref, att_ref, inv_ref,
-                   own_s, G, XR, P3, pad_s, mask_s, t_s, w_s, vv_s, dm_s, snd, rcv, hsnd, hrcv, dsnd, drcv, osem):
+                   own_s, G, XR, P3, pad_s, mask_s, t_s, w_s, vv_s, dm_s, snd, rcv, hsnd, hrcv, dsnd, drcv, osem, vb_s):
     S, W = x_ref.shape
     f = wo_ref.shape[0]
     win = bias_ref.shape[1]
@@ -581,9 +582,12 @@
         return jnp.concatenate([v[:, t * W + j * wide:t * W + (j + 1) * wide] for t in range(3)], 1)
 
     wq = wq_ref[...].astype(F32)
-    b3 = placed(b3_ref[...], 3 * f)
-    b4 = placed(b4_ref[...], 4 * f)
-    singles = pltpu.roll(b1_ref[...], p.me * f, 1)
+    vb_s[...] = jnp.zeros_like(vb_s)
+    for i, r in enumerate((vq_ref, vu_ref, v1_ref, v2_ref, v3_ref, v4_ref, v5_ref, v6_ref)):
+        vb_s[i:i + 1, :r.shape[1]] = r[...].astype(F32)
+    b3 = placed(vb_s[0:1, :3 * W], 3 * f)
+    b4 = placed(vb_s[1:2, :], 4 * f)
+    singles = pltpu.roll(vb_s[:, :W], p.me * f, 1)[2:8]
     rest = [[b4[:, j * W:(j + 1) * W] for j in range(4)] + [singles[0:3]], [singles[3:6], jnp.zeros((4, W), F32)], [jnp.zeros((7, W), F32)]]
     for j in range(3):
         own_s[j * SLAB:(j + 1) * SLAB, :] = jnp.concatenate([thirds(wq, j), thirds(b3, j)] + rest[j], 0).astype(BF16)
@@ -773,7 +777,7 @@
     vec_ref[8 * j:8 * j + 8, :] = lax.fori_loop(0, 4 * G.shape[0], one, jnp.zeros((SLAB - f, G.shape[-1]), F32))
 
 
-def forward(n_seq, wq, wo, wu, wd, b3, b4, b1, x, pad, bias, draws, lens):
+def forward(n_seq, wq, wo, wu, wd, vectors, x, pad, bias, draws, lens):
     S, W = x.shape
     f = wo.shape[0]
     win = bias.shape[1]
@@ -793,14 +797,14 @@
     return pl.pallas_call(
         functools.partial(forward_kernel, n_seq, chunks, dims ** -0.25),
         out_shape=large + (sd((24, W), F32), sd((1, KS), jnp.int32), sd((Z, 4 * f, W), BF16)),
-        in_specs=vmem(11) + [pl.BlockSpec(memory_space=pltpu.SMEM)], out_specs=(pl.BlockSpec(memory_space=pl.ANY),) * len(large) + tuple(vmem(3)),
+        in_specs=vmem(16) + [pl.BlockSpec(memory_space=pltpu.SMEM)], out_specs=(pl.BlockSpec(memory_space=pl.ANY),) * len(large) + tuple(vmem(3)),
         scratch_shapes=[V(s.shape, s.dtype) for s in large] + [
             V((R, W), BF16), V((Z, 2, 2, 2, R, W), BF16), V((S, W), BF16), V((3, 8, S), jnp.int32), V((8, S), jnp.int32),
-            V((S, span), F32), V((2 * SB, span), F32), V((2 * SB, span), BF16), V((KS, 256), BF16),
-            V((2, heads // 2, 2 * feats, 2 * dims), BF16), dma(K, M), dma(K, M), dma(6), dma(6), dma(Z - 1), dma(Z - 1), dma(24)],
+            V((S, span), F32), V((2 * SB, span), F32), V((2, 2 * SB, span), BF16), V((KS, 256), BF16),
+            V((2, heads // 2, 2 * feats, 2 * dims), BF16), dma(K, M), dma(K, M), dma(6), dma(6), dma(Z - 1), dma(Z - 1), dma(24), V((8, 4 * W), F32)],
         compiler_params=pltpu.CompilerParams(collective_id=1, has_side_effects=True, vmem_limit_bytes=60 << 20),
         name="forward",
-    )(wq, wo, wu, wd, b3, b4, b1, x, pad, bias, draws, lens)
+    )(wq, wo, wu, wd, *vectors, x, pad, bias, draws, lens)
 
 
 DOWN_PARTS = 3
@@ -839,7 +843,7 @@
     FF_ = up_ref.shape[1]
     n_dev = P_ref.shape[0]
     f = W // n_dev
-    RB = 64
+    RB = 256
     p = Place(n_seq)
     loads = [pltpu.make_async_copy(a, b, lsem.at[i]) for i, (a, b) in enumerate(
         ((att_h, att_ref), (ow_h, ow_ref), (up_h, up_ref), (ct_h, ct_ref), (inv_h, inv_ref)))]
@@ -970,7 +974,7 @@
         gt_ref[rs, :] = (hi + pltpu.roll(total - hi, heads, 1)).astype(BF16)
 
     loads[4].wait()
-    rows_loop(S, 2 * RB, weighted)
+    rows_loop(S, RB, weighted)
     g.drain()
     for c in leaving:
         c.wait()
@@ -998,11 +1002,11 @@
 
 
 BACKWARD = (
-    "H0", "b3", "b0", "b1", "pre0", "c0", "b4", "pr2", "c1", "o0", "b2", "c2", "pr1", "pr0", "hw0", "o1", "v0", "c3", "ri0",
-    "t0", "o2", "t1", "pj0", "c4", "b5", "o3", "ri1", "t2", "c5", "pj1", "v1", "b6", "o4", "f1", "t3", "o5", "c6", "f0", "ri2",
-    "t4", "pj2", "b7", "v2", "t5", "o6", "c7", "t6", "v3", "f3", "o7", "t7", "f5", "v4", "f6", "f2", "f4", "gx0", "f7", "v5",
+    "b0", "b1", "H0", "pre0", "c0", "pr0", "c1", "b2", "pr1", "o0", "c2", "pr2", "b4", "hw0", "o1", "b3", "ri0", "v0", "c3",
+    "t0", "o2", "pj0", "c4", "b5", "v1", "t1", "ri1", "o3", "t2", "pj1", "c5", "b6", "o4", "t3", "ri2", "o5", "t4", "c6", "pj2",
+    "b7", "t5", "v2", "o6", "v3", "c7", "t6", "f2", "v4", "f1", "o7", "f5", "t7", "f3", "f0", "gx0", "f4", "f6", "v5", "f7",
 )
-CUT_BACKWARD = (32, 32, 32, 32, 16, 16, 16, 16)
+CUT_BACKWARD = (48, 32, 32, 32, 16, 16, 16, 16)
 
 
 def head_rows(gw, gt, i, heads):
@@ -1301,6 +1305,22 @@
         name="backward",
     )(x, pk, bias, draws, lens, vg, gw, gt, w, q, k, v, zq, zk, g1, P_)
 
+
+def finish_kernel(n, small_ref, *refs):
+    for src, dst in zip(refs[:n], refs[n:2 * n]):
+        dst[...] = src[...]
+    for i, v in enumerate(refs[2 * n:]):
+        v[...] = small_ref[i:i + 1, :v.shape[1]]
+
+
+def finish(f, small, *large):
+    sd = jax.ShapeDtypeStruct
+    return pl.pallas_call(
+        functools.partial(finish_kernel, len(large)),
+        out_shape=tuple(sd(a.shape, a.dtype) for a in large) + tuple(sd((1, n), F32) for n in (3 * f, 4 * f) + (f,) * 6),
+        name="finish",
+    )(small, *large)
+
 EPS = 1e-06
 EXACT_MATMUL = lax.Precision.HIGHEST
 
@@ -1359,19 +1379,17 @@
     W = local.shape[1]
     n_seq = lax.axis_size("seq")
     f = w_out.shape[0]
-    b3 = jnp.pad(b_qkv.astype(F32), (0, 3 * W - 3 * f))[None]
-    b4 = jnp.pad(b_up.astype(F32), (0, 4 * W - 4 * f))[None]
-    b1 = jnp.pad(jnp.stack([b_out, gain_a, shift_a, b_down, gain_f, shift_f]).astype(F32), ((0, 2), (0, W - f)))
+    vectors = [v[None] for v in (b_qkv, b_up, b_out, gain_a, shift_a, b_down, gain_f, shift_f)]
     (qkv_w, out_w, up_w, zq, zk, q, k, v, att, inv, vec, pk, col) = forward(
-        n_seq, w_qkv, w_out, w_up, w_down, b3, b4, b1, local, padding, rel_bias, feature_draws, lengths)
+        n_seq, w_qkv, w_out, w_up, w_down, vectors, local, padding, rel_bias, feature_draws, lengths)
     out, g1, gw, gt, vg, P_ = middle(n_seq, rel_bias.shape[0], col, local, cotangent[0], att, inv, out_w, up_w, vec)
     P_ = P_.reshape(n_seq // 2, 2, 2, P_.shape[1], W)
     gx, rel, g_qkv, g_up, g_down, g_out, small = backward(
         n_seq, local, pk, rel_bias, feature_draws, lengths, qkv_w, q, k, v, vg, zq, zk, gw, gt, g1, P_)
-    one = [small[i, :f] for i in range(2, 8)]
+    out, gx, rel, g_qkv, g_up, g_down, g_out, *vec = finish(f, small, out, gx, rel, g_qkv, g_up, g_down, g_out)
+    vec = [v[0] for v in vec]
     return (
-        out[None], gx[None], rel, g_qkv, small[0, : 3 * f], g_out, one[0], one[1], one[2], g_up, small[1, : 4 * f],
-        g_down, one[3], one[4], one[5],
+        out[None], gx[None], rel, g_qkv, vec[0], g_out, vec[2], vec[3], vec[4], g_up, vec[1], g_down, vec[5], vec[6], vec[7],
     )
 
 

time: 261 us -> 233 us (0.89)
  Pallas kernels: 241 us -> 228 us
  local copies, waits for them, and re-layouts: 11.9 us -> 0 us
    pallas_call x1, Pallas kernels: 107 us -> 95.8 us  [backward(): pl.pallas_call(functools.partial(backward_kernel, n_seq, chunks, dims **...]
    unnamed x19 -> x0, local copies, waits for them, and re-layouts: 6.61 us -> none
    squeeze x3 -> x0, local copies, waits for them, and re-layouts: 3.91 us -> none  [the longest x1 1.42 us: with_kernels(): one = [small[i, :f] for i in range(2, 8)]]
    pallas_call x0 -> x1, Pallas kernels: none -> 3.71 us  [finish(): pl.pallas_call(functools.partial(finish_kernel, len(large)), out_shape=tu...]
    pallas_call x1, Pallas kernels: 53.2 us -> 49.5 us  [middle(): pl.pallas_call(functools.partial(middle_kernel, n_seq, heads), out_shape=...]
where the time goes in v3:
time: 233 us; the launch traced here: 229 us
  Pallas kernels  228 us (98%)
    pallas_call x1, Pallas kernels, backward(): pl.pallas_call(functools.partial(backward_kernel, n_seq, chunks, dims **...  95.8 us
    pallas_call x1, Pallas kernels, forward(): pl.pallas_call(functools.partial(forward_kernel, n_seq, chunks, dims ** (...  78.8 us
    pallas_call x1, Pallas kernels, middle(): pl.pallas_call(functools.partial(middle_kernel, n_seq, heads), out_shape=...  49.5 us

profile of v3, /device:TPU:0, one launch (start us, length us, event | category | flops | bytes accessed | tf_op | source)
XLA Modules:
  0.0 228.7 jit_solution(15253669364760553543)
XLA Ops:
  0.7 78.8 %forward.1 = (bf16[3,768,768]{2,1,0:T(8,128)(2,1)}, bf16[768,768]{1,0:T(8,128)(2,1)}, bf16[768,3072]{1,0:T(8,128)(2,1)}, f32[512,768]{1,0:T(8,128)}, f32[512,768...) custom-call(bf16[24,2304]{1,0:T(8,128)(2,1)} %wq_ref.1, ...), custom_call_target="tpu_custom_call" | custom-call | tf_op jit(solution)/shard_map/forward/pallas_call | solution.py:797
  79.4 49.5 %middle.1 = (bf16[512,768]{1,0:T(8,128)(2,1)}, f32[512,768]{1,0:T(8,128)}, bf16[512,768]{1,0:T(8,128)(2,1)}, bf16[512,128]{1,0:T(8,128)(2,1)}, f32[24,768]{1,0:T(8,128)}, /*index=5*/bf16[32,224,768]{2,1,0:T(8,128)(2,1)}) custom-call(bf16[4,96,768]{2,1,0:T(8,128)(2,1)} %get-tuple-element.57.col_ref, bf16[512,768]{1,0:T(8,128)(2,1)} %bitcast.23, ...), custom_call_target="tpu_custom_call" | custom-call | tf_op jit(solution)/shard_map/middle/pallas_call | solution.py:991
  129.0 95.8 %backward.1 = (f32[512,768]{1,0:T(8,128)}, f32[12,1024]{1,0:T(8,128)}, f32[24,2304]{1,0:T(8,128)}, f32[24,3072]{1,0:T(8,128)}, f32[96,768]{1,0:T(8,128)}, /*index=5*/f32[24,768]{1,0:T(8,128)}, f32[8,128]{1,0:T(8,128)}) custom-call(bf16[512,768]{1,0:T(8,128)(2,1)} %bitcast.24, s32[1,1536]{1,0:T(1,128)} %get-tuple-element.56.pk_ref, f32[12,1024]{1,0:T(8,128)} %bias_ref.3, ...), custom_call_target="tpu_custom_call" | custom-call | tf_op jit(solution)/shard_map/backward/pallas_call | solution.py:1293
  224.8 3.7 %finish.1 = (bf16[512,768]{1,0:T(8,128)(2,1)}, f32[512,768]{1,0:T(8,128)}, f32[12,1024]{1,0:T(8,128)}, f32[24,2304]{1,0:T(8,128)}, f32[24,3072]{1,0:T(8,128)}, /...) custom-call(f32[8,128]{1,0:T(8,128)} %get-tuple-element.74.small_ref, ...), custom_call_target="tpu_custom_call" | custom-call | tf_op jit(solution)/shard_map/finish/pallas_call | solution.py:1318

commit v4 on v3

--- a/solution.py
+++ b/solution.py
@@ -1307,19 +1307,35 @@
 
 
 def finish_kernel(n, small_ref, *refs):
-    for src, dst in zip(refs[:n], refs[n:2 * n]):
+    for src, dst in zip(refs[:2], refs[n:n + 2]):
         dst[...] = src[...]
-    for i, v in enumerate(refs[2 * n:]):
-        v[...] = small_ref[i:i + 1, :v.shape[1]]
+
+    @pl.when(pl.program_id(0) == 0)
+    def _():
+        for src, dst in zip(refs[2:n], refs[n + 2:2 * n]):
+            dst[...] = src[...]
+        for i, v in enumerate(refs[2 * n:]):
+            v[...] = small_ref[i:i + 1, :v.shape[1]]
 
 
 def finish(f, small, *large):
     sd = jax.ShapeDtypeStruct
+    steps = 4
+
+    def whole(shape):
+        return pl.BlockSpec(shape, lambda i: (0, 0))
+
+    specs = [pl.BlockSpec((a.shape[0] // steps, a.shape[1]), lambda i: (i, 0)) for a in large[:2]] + [whole(a.shape) for a in large[2:]]
+    vectors = [(1, n) for n in (3 * f, 4 * f) + (f,) * 6]
     return pl.pallas_call(
         functools.partial(finish_kernel, len(large)),
-        out_shape=tuple(sd(a.shape, a.dtype) for a in large) + tuple(sd((1, n), F32) for n in (3 * f, 4 * f) + (f,) * 6),
+        grid=(steps,),
+        out_shape=tuple(sd(a.shape, a.dtype) for a in large) + tuple(sd(v, F32) for v in vectors),
+        in_specs=[whole(small.shape)] + specs,
+        out_specs=tuple(specs) + tuple(whole(v) for v in vectors),
         name="finish",
     )(small, *large)
+
 
 EPS = 1e-06
 EXACT_MATMUL = lax.Precision.HIGHEST

time: 233 us -> 234 us (level)
  no operation moved by 1% of the time
where the time goes in v4:
time: 234 us; the launch traced here: 230 us
  Pallas kernels  229 us (98%)
    pallas_call x1, Pallas kernels, backward(): pl.pallas_call(functools.partial(backward_kernel, n_seq, chunks, dims **...  95.8 us
    pallas_call x1, Pallas kernels, forward(): pl.pallas_call(functools.partial(forward_kernel, n_seq, chunks, dims ** (...  78.8 us
    pallas_call x1, Pallas kernels, middle(): pl.pallas_call(functools.partial(middle_kernel, n_seq, heads), out_shape=...  49.5 us

profile of v4, /device:TPU:0, one launch (start us, length us, event | category | flops | bytes accessed | tf_op | source)
XLA Modules:
  0.0 229.7 jit_solution(14829227931528180100)
XLA Ops:
  0.7 78.8 %forward.1 = (bf16[3,768,768]{2,1,0:T(8,128)(2,1)}, bf16[768,768]{1,0:T(8,128)(2,1)}, bf16[768,3072]{1,0:T(8,128)(2,1)}, f32[512,768]{1,0:T(8,128)}, f32[512,768...) custom-call(bf16[24,2304]{1,0:T(8,128)(2,1)} %wq_ref.1, ...), custom_call_target="tpu_custom_call" | custom-call | tf_op jit(solution)/shard_map/forward/pallas_call | solution.py:797
  79.4 49.5 %middle.1 = (bf16[512,768]{1,0:T(8,128)(2,1)}, f32[512,768]{1,0:T(8,128)}, bf16[512,768]{1,0:T(8,128)(2,1)}, bf16[512,128]{1,0:T(8,128)(2,1)}, f32[24,768]{1,0:T(8,128)}, /*index=5*/bf16[32,224,768]{2,1,0:T(8,128)(2,1)}) custom-call(bf16[4,96,768]{2,1,0:T(8,128)(2,1)} %get-tuple-element.57.col_ref, bf16[512,768]{1,0:T(8,128)(2,1)} %bitcast.23, ...), custom_call_target="tpu_custom_call" | custom-call | tf_op jit(solution)/shard_map/middle/pallas_call | solution.py:991
  129.0 95.8 %backward.1 = (f32[512,768]{1,0:T(8,128)}, f32[12,1024]{1,0:T(8,128)}, f32[24,2304]{1,0:T(8,128)}, f32[24,3072]{1,0:T(8,128)}, f32[96,768]{1,0:T(8,128)}, /*index=5*/f32[24,768]{1,0:T(8,128)}, f32[8,128]{1,0:T(8,128)}) custom-call(bf16[512,768]{1,0:T(8,128)(2,1)} %bitcast.24, s32[1,1536]{1,0:T(1,128)} %get-tuple-element.56.pk_ref, f32[12,1024]{1,0:T(8,128)} %bias_ref.3, ...), custom_call_target="tpu_custom_call" | custom-call | tf_op jit(solution)/shard_map/backward/pallas_call | solution.py:1293
  224.8 4.7 %finish.1 = (bf16[512,768]{1,0:T(8,128)(2,1)}, f32[512,768]{1,0:T(8,128)}, f32[12,1024]{1,0:T(8,128)}, f32[24,2304]{1,0:T(8,128)}, f32[24,3072]{1,0:T(8,128)}, /...) custom-call(f32[8,128]{1,0:T(8,128)} %get-tuple-element.74.small_ref, ...), custom_call_target="tpu_custom_call" | custom-call | tf_op jit(solution)/shard_map/finish/pallas_call | solution.py:1330
